TPU v7x, 128 devices: a whole 4x4x4 slice. The times are simulated.
128 devices in a mesh: outer: 8 (over z_hi, y), inner: 16 (over z_lo, x, core).
Axes of the slice: x: 4, y: 4, z: 4 (z_hi: 2, z_lo: 2; z = z_hi * 2 + z_lo), core: 2. Of those that a mesh axis runs over, the one named last changes fastest.
Arguments:
- queries: bfloat16 [32768, 2560], P(('outer', 'inner')), may hold values from -6 to 6
- keys: bfloat16 [32768, 2560], P(('outer', 'inner')), may hold values from -6 to 6
- values: bfloat16 [32768, 2560], P(('outer', 'inner')), may hold values from -6 to 6
- latents: bfloat16 [4096, 3, 2560], P(('outer', 'inner')), may hold values from -6 to 6
- latent_owner: int32 [1024], P(('outer', 'inner')), may hold values from 0 to 15, as said below
- token_source: int32 [32768], P(('outer', 'inner')), may hold values from -1 to 63, as said below
- doc_lengths: int32 [64], replicated, may hold values from 1 to 2048, 32768 in all
Outputs:
- attended: bfloat16 [32768, 2560], P(('outer', 'inner'))
Inputs may be any that keep to these rules, and one draw needn't show every extreme that they name: `latent_owner`: the 8 images of one device go to distinct devices of its outer group, so at most 4 latent rows go from one device to one other; in every outer group some device receives an image from every device of the group. `token_source`: consistent with latent_owner: each image sent to a device fills 4 consecutive positions of that device's block, starting at a multiple of 4, in the order of its rows; every image fills exactly one such run.
All inputs are finite; a program needn't handle non-finite values.
Results may differ from a plain program's by a relative error of at most 0.004.
Values may be sent and summed in bfloat16 or wider, within the bound.
No kernel may reach another device: no remote copies, remote signals or barrier semaphores. Data moves between devices by JAX's collectives and lax.ppermute only.
A program may use at most 64 MiB of HBM per device.

v0:
```python
import functools

import jax
import jax.numpy as jnp
from jax import lax
from jax.experimental import pallas as pl
from jax.experimental.pallas import tpu as pltpu
from jax.sharding import PartitionSpec as P

HEADS = 20
HEAD = 128
ROWS = 256
XS = 4
GROUP = HEADS // XS
WIDTH = GROUP * HEAD
BLOCKS = 8
LATENTS = 32
AXES = ("outer", "inner")
CHUNKS = ((0, 3), (3, 2))
UNROLL = 4
SLOTS = XS * (BLOCKS + 1) + 3 * UNROLL

SCALE = HEAD ** (-0.5) * 1.4426950408889634
HIDDEN = -1e30
HALVES = (slice(0, HEAD), slice(HEAD, ROWS))
MIB = 1024 * 1024
SLAB = (ROWS, HEAD)


def routes(target):
    return [(d, target(d)) for d in range(128) if 0 <= target(d) < 128]


def along_x(steps):
    return routes(lambda d: (d & ~7) | ((d + 2 * steps) & 7))


TO_CORE = routes(lambda d: d ^ 1)
TO_Z = routes(lambda d: d ^ 8)
TO_NEXT = routes(lambda d: d + 8)


def send(value, route):
    return lax.ppermute(value, AXES, route)


def across_x(parts):
    return [parts[0]] + [send(parts[XS - rel], along_x(XS - rel)) for rel in range(1, XS)]


def params(mib):
    return pltpu.CompilerParams(vmem_limit_bytes=mib * MIB)


ANY = pl.BlockSpec(memory_space=pl.ANY)
HBM = pl.BlockSpec(memory_space=pltpu.HBM)
SMEM = pl.BlockSpec(memory_space=pltpu.SMEM)
VMEM = pl.BlockSpec(memory_space=pltpu.VMEM)


def in_hbm(value):
    return pltpu.with_memory_space_constraint(value, pltpu.HBM)


def start_copies(copies, sems, first=0):
    started = [pltpu.make_async_copy(a, b, sems.at[first + n]) for n, (a, b) in enumerate(copies)]
    for copy in started:
        copy.start()
    return started


def wait_for(copies):
    for copy in copies:
        copy.wait()


def pack_kernel(parcels, small, order, place, owner, *refs):
    count = len(order)
    tensors = dict(zip(order, refs[:count]))
    refs = refs[count:]
    outs, sems = refs[: len(parcels) * XS], refs[-1]
    refs = refs[len(parcels) * XS : -1]
    copies, later = [], []
    for rel in range(XS):
        column = ((place[0] + rel) & 3) * WIDTH

        def cut(head):
            return pl.ds(pl.multiple_of(column + head * HEAD, HEAD), HEAD)

        if small:
            for s, (kind, head) in enumerate(small):
                copies.append((tensors["latents"].at[kind, :, cut(head)], refs[rel].at[2 + s]))
            later.append((refs[XS], refs[rel].at[pl.ds(0, 2)]))
        for n, parcel in enumerate(parcels):
            for s, slab in enumerate(parcel):
                target = outs[n * XS + rel].at[s]
                copies.append((tensors[slab[0]].at[:, cut(slab[1])], target))
    if small:
        notes, sources, owned = refs[XS:]
        fetched = start_copies([(owner, owned), (tensors["sources"], sources)], sems)
    started = start_copies(copies, sems, 2 if small else 0)
    if small:
        wait_for(fetched)
        row = lax.broadcasted_iota(jnp.int32, (LATENTS, HEAD), 0)
        wide = jnp.where(row == 0, sources[0:1], jnp.where(row == 1, sources[1:2], 0))
        notes[0] = wide.astype(jnp.float32).astype(jnp.bfloat16)
        owners = jnp.zeros((LATENTS, HEAD), jnp.int32)
        for image in range(LATENTS // 4):
            owners = jnp.where(row // 4 == image, owned[image], owners)
        notes[1] = owners.astype(jnp.float32).astype(jnp.bfloat16)
        started += start_copies(later, sems, 2 + len(copies))
    wait_for(started)


def pack(place, owner, tensors, parcels, small=()):
    order = tuple(tensors)
    shapes = [jax.ShapeDtypeStruct((len(parcel),) + SLAB, jnp.bfloat16) for parcel in parcels for _ in range(XS)]
    count = XS * sum(len(parcel) for parcel in parcels)
    scratch = []
    if small:
        shapes += [jax.ShapeDtypeStruct((2 + len(small), LATENTS, HEAD), jnp.bfloat16)] * XS
        count += XS * (len(small) + 1) + 2
        scratch = [
            pltpu.VMEM((2, LATENTS, HEAD), jnp.bfloat16),
            pltpu.VMEM((2, HEAD), jnp.int32),
            pltpu.SMEM(owner.shape, jnp.int32),
        ]
    given = [in_hbm(tensor) for tensor in (owner, *tensors.values())]
    outs = pl.pallas_call(
        functools.partial(pack_kernel, parcels, small, order),
        out_shape=shapes,
        in_specs=[SMEM] + [HBM] * len(given),
        out_specs=[ANY] * len(shapes),
        scratch_shapes=scratch + [pltpu.SemaphoreType.DMA((count,))],
        compiler_params=params(2),
    )(place, *given)
    return [outs[n : n + XS] for n in range(0, len(outs), XS)]


def marks_kernel(place, near, near_z, far, far_z, hot, keep):
    x, core, z = place[0], place[1], place[2]
    pieces = [source[r, 1] for source in (near, near_z, far, far_z) for r in range(XS)]
    owners = jnp.concatenate(pieces, axis=0).astype(jnp.float32).T[0:1]
    lane = lax.broadcasted_iota(jnp.int32, (1, 4 * XS * LATENTS), 1)
    from_x = (x + ((lane >> 5) & 3)) & 3
    sender = ((z ^ ((lane >> 7) & 1)) * 8) + from_x * 2 + (core ^ (lane >> 8))
    code = (sender * 4 + (lane & 3)).astype(jnp.float32)
    for rel in range(XS):
        block = (z * 8 + ((x + rel) & 3) * 2 + core).astype(jnp.float32)
        sources = jnp.concatenate([near[rel, 0, 0:1], near[rel, 0, 1:2]], axis=1).astype(jnp.float32)
        sources = jnp.broadcast_to(sources, (HEAD, ROWS)).T
        wanted = jnp.where(owners == block, code, -2.0)
        for tile in range(4):
            lanes = slice(tile * HEAD, (tile + 1) * HEAD)
            hot[rel, :, lanes] = jnp.where(sources == wanted[:, lanes], 1.0, 0.0).astype(jnp.bfloat16)
        keep[rel] = jnp.where(sources < 0, 1.0, 0.0).astype(jnp.bfloat16)


def marks(place, lat):
    return pl.pallas_call(
        marks_kernel,
        out_shape=[
            jax.ShapeDtypeStruct((XS, ROWS, 4 * XS * LATENTS), jnp.bfloat16),
            jax.ShapeDtypeStruct((XS,) + SLAB, jnp.bfloat16),
        ],
        in_specs=[SMEM] + [VMEM] * 4,
        out_specs=[VMEM] * 2,
        compiler_params=params(8),
    )(place, *lat)


def merge_kernel(base, work, *refs):
    parts, lats, (hot, keep, out, raw, lat, sems) = refs[:XS], refs[XS : XS + 4], refs[XS + 4 :]
    count = len(work)
    copies = [(parts[rel].at[pl.ds(base, count)], raw.at[rel]) for rel in range(XS)]
    started = start_copies([(lats[n], lat.at[n]) for n in range(4)] + copies, sems)
    wait_for(started)
    for n in range(0, count, 2):
        pair = work[n : n + 2]
        columns = [
            jnp.concatenate([lat[g, r, slot] for g in range(4) for r in range(XS)], axis=0) for _, slot in pair
        ]
        columns = jnp.concatenate(columns, axis=1)
        for rel in range(XS):
            kept = keep[rel] > 0
            placed = jnp.dot(hot[rel], columns, preferred_element_type=jnp.float32)
            for p, (kind, _) in enumerate(pair):
                mixed = placed[:, p * HEAD : (p + 1) * HEAD]
                mixed = jnp.where(kept, raw[rel, n + p].astype(jnp.float32), mixed)
                if kind == 2:
                    mixed = jnp.concatenate([mixed[:HEAD].T, mixed[HEAD:].T], axis=0)
                out[rel, n + p] = mixed.astype(jnp.bfloat16)


def merge(parts, base, lat, hot, keep, work):
    count = len(work)
    return pl.pallas_call(
        functools.partial(merge_kernel, base, work),
        out_shape=jax.ShapeDtypeStruct((XS, count) + SLAB, jnp.bfloat16),
        in_specs=[ANY] * (XS + 4) + [VMEM] * 2,
        out_specs=VMEM,
        scratch_shapes=[
            pltpu.VMEM((XS, count) + SLAB, jnp.bfloat16),
            pltpu.VMEM((4,) + lat[0].shape, jnp.bfloat16),
            pltpu.SemaphoreType.DMA((XS + 4,)),
        ],
        compiler_params=params(10),
    )(*parts, *lat, hot, keep)


def plan_kernel(place, lengths, begins, items):
    x, core, z, outer = place[0], place[1], place[2], place[3]
    origin = (outer * 16 + z * 8 - BLOCKS) * ROWS
    mine = [BLOCKS + 2 * ((x + rel) & 3) + core for rel in range(XS)]
    column = lax.broadcasted_iota(jnp.int32, (8, ROWS), 1)
    zero = jnp.zeros((8, ROWS), jnp.int32) - origin

    def document(d, carry):
        start, firsts, lasts, vectors = carry
        at = start - origin
        firsts = [jnp.where(at <= mine[r] * ROWS, at, firsts[r]) for r in range(XS)]
        lasts = [jnp.where(at <= mine[r] * ROWS + ROWS - 1, at, lasts[r]) for r in range(XS)]
        vectors = [jnp.where(at <= mine[r] * ROWS + column, at, vectors[r]) for r in range(XS)]
        return start + lengths[d], firsts, lasts, vectors

    least = [-origin] * XS
    _, firsts, lasts, vectors = lax.fori_loop(
        0, lengths.shape[0], document, (jnp.int32(0), least, least, [zero] * XS)
    )
    for rel in range(XS):
        begins[rel] = vectors[rel][0:1]

    def held(j):
        return jnp.where(j < BLOCKS, 8, 0) + ((j & 1) ^ core) * 4 + (((j >> 1) - x) & 3)

    def listed(count, low, high):
        for rel in range(XS):

            def add(j, count, rel=rel):
                items[0, count] = rel
                items[1, count] = j
                items[2, count] = held(j)
                return count + 1

            count = lax.fori_loop(low[rel], high[rel], add, count)
        for extra in range(UNROLL - 1):
            items[0, count + extra] = XS
            items[1, count + extra] = BLOCKS
            items[2, count + extra] = spare
        return (count + UNROLL - 1) // UNROLL * UNROLL

    for rel in range(XS):
        items[0, rel] = rel
        items[1, rel] = mine[rel]
        items[2, rel] = rel
    low = [first // ROWS for first in firsts]
    clear = [jnp.clip((last + ROWS - 1) // ROWS, BLOCKS, mine[rel]) for rel, last in enumerate(lasts)]
    spare = 0
    edge = listed(XS, [jnp.maximum(at, BLOCKS) for at in low], clear)
    end = listed(edge, clear, mine)
    spare = 2 * XS
    items[3, 0] = edge
    items[3, 1] = end
    items[3, 2] = listed(end, low, [BLOCKS] * XS)


def plan(place, lengths):
    return pl.pallas_call(
        plan_kernel,
        out_shape=[
            jax.ShapeDtypeStruct((XS, 1, ROWS), jnp.int32),
            jax.ShapeDtypeStruct((4, SLOTS + UNROLL), jnp.int32),
        ],
        in_specs=[SMEM, SMEM],
        out_specs=[VMEM, SMEM],
        compiler_params=params(2),
    )(place, lengths)


def attend_kernel(part, query_at, slab_at, state_at, heads, items, begins, q_hbm, *refs):
    sources = 4 if part == "all" else 2
    lowest = 2 if part == "before" else 0
    kept, refs = refs[:sources], refs[sources:]
    if part == "before":
        state, refs = refs[:3], refs[3:]
    count = 3 if part == "own" else XS
    outs, (q_buf, kv_buf, scores, best, total, accum, sems) = refs[:count], refs[count:]
    copies = [(q_hbm.at[:, pl.ds(query_at, heads)], q_buf)]
    copies += [(source.at[:, pl.ds(slab_at, 2 * heads)], kv_buf.at[n]) for n, source in enumerate(kept)]
    wait_for(start_copies(copies, sems))
    edge, end, last = items[3, 0], items[3, 1], items[3, 2]
    begin = end if part == "before" else 0
    stop = end if part == "own" else last

    key_row = lax.broadcasted_iota(jnp.int32, (ROWS, ROWS), 0)
    query_column = lax.broadcasted_iota(jnp.int32, (ROWS, ROWS), 1)

    for h in range(heads):
        best[...] = jnp.full(best.shape, HIDDEN, jnp.float32)
        total[...] = jnp.zeros(total.shape, jnp.float32)
        accum[...] = jnp.zeros(accum.shape, jnp.float32)
        if part == "before":
            for q in range(XS):
                best[q] = state[0][state_at + h, q]

        def score(slot, masked, diagonal):
            q, j, at = items[0, slot], items[1, slot], items[2, slot] - lowest * XS
            tile = lax.dot_general(
                kv_buf[at >> 2, at & 3, 2 * h],
                q_buf[q & 3, h],
                (((1,), (1,)), ((), ())),
                preferred_element_type=jnp.float32,
            )
            if masked:
                seen = key_row >= begins[q & 3] - j * ROWS
                if diagonal:
                    seen = seen & (key_row <= query_column)
                tile = jnp.where(seen, tile, HIDDEN)
            scores[slot] = tile
            best[q] = jnp.maximum(best[q], jnp.max(tile.reshape(ROWS // 8, 8, ROWS), axis=0))

        def weigh(slot):
            q, at = items[0, slot], items[2, slot] - lowest * XS
            weights = jnp.exp2(scores[slot] * SCALE - best[q, 0:1])
            total[q] = total[q] + jnp.sum(weights.reshape(ROWS // 8, 8, ROWS), axis=0)
            value = jnp.concatenate([kv_buf[at >> 2, at & 3, 2 * h + 1, half] for half in HALVES], axis=1)
            accum[q] = accum[q] + jnp.dot(value, weights.astype(jnp.bfloat16), preferred_element_type=jnp.float32)

        def grouped(low, high, one):
            def several(n, carry):
                for extra in range(UNROLL):
                    one(low + n * UNROLL + extra)
                return carry

            lax.fori_loop(0, (high - low) // UNROLL, several, 0)

        if part != "before":
            for rel in range(XS):
                score(rel, True, True)
            grouped(XS, edge, lambda slot: score(slot, True, False))
            grouped(edge, end, lambda slot: score(slot, False, False))
        if part != "own":
            grouped(end, last, lambda slot: score(slot, True, False))
        for q in range(XS + 1):
            top = jnp.max(best[q], axis=0, keepdims=True)
            if part == "before" and q < XS:
                shrink = jnp.exp2((state[0][state_at + h, q, 0:1] - top) * SCALE)
                total[q] = state[1][state_at + h, q] * shrink
                accum[q] = state[2][state_at + h, q] * shrink
            if part == "own" and q < XS:
                outs[0][h, q] = jnp.broadcast_to(top, (8, ROWS))
            best[q] = jnp.broadcast_to(top * SCALE, (8, ROWS))
        grouped(begin, stop, weigh)
        for rel in range(XS):
            if part == "own":
                outs[1][h, rel] = total[rel]
                outs[2][h, rel] = accum[rel]
            else:
                mixed = accum[rel] / jnp.sum(total[rel], axis=0, keepdims=True)
                outs[rel][h] = mixed.T.astype(jnp.bfloat16)


def attend(part, planned, query, sources, heads, query_at=0, head_at=0, state=()):
    begins, items = planned
    if part == "own":
        shapes = [(heads, XS, 8, ROWS), (heads, XS, 8, ROWS), (heads, XS, HEAD, ROWS)]
        shapes = [jax.ShapeDtypeStruct(shape, jnp.float32) for shape in shapes]
    else:
        shapes = [jax.ShapeDtypeStruct((heads,) + SLAB, jnp.bfloat16)] * XS
    return pl.pallas_call(
        functools.partial(attend_kernel, part, query_at, 2 * head_at, head_at, heads),
        out_shape=shapes,
        in_specs=[SMEM, VMEM] + [ANY] * (1 + len(sources)) + [VMEM] * len(state),
        out_specs=[VMEM] * len(shapes),
        scratch_shapes=[
            pltpu.VMEM((XS, heads) + SLAB, jnp.bfloat16),
            pltpu.VMEM((len(sources), XS, 2 * heads) + SLAB, jnp.bfloat16),
            pltpu.VMEM((SLOTS, ROWS, ROWS), jnp.float32),
            pltpu.VMEM((XS + 1, 8, ROWS), jnp.float32),
            pltpu.VMEM((XS + 1, 8, ROWS), jnp.float32),
            pltpu.VMEM((XS + 1, HEAD, ROWS), jnp.float32),
            pltpu.SemaphoreType.DMA((5,)),
        ],
        compiler_params=params(24 + 2 * heads),
    )(items, begins, query, *sources, *state)


def unpack_kernel(chunks, place, *refs):
    parts, out, sems = refs[: len(chunks) * XS], refs[-2], refs[-1]
    copies = []
    for n, (first, heads) in enumerate(chunks):
        for rel in range(XS):
            for h in range(heads):
                begin = pl.multiple_of(((place[0] + rel) & 3) * WIDTH + (first + h) * HEAD, HEAD)
                copies.append((parts[n * XS + rel].at[h], out.at[:, pl.ds(begin, HEAD)]))
    wait_for(start_copies(copies, sems))


def unpack(place, parts, chunks, before=()):
    return pl.pallas_call(
        functools.partial(unpack_kernel, chunks),
        out_shape=jax.ShapeDtypeStruct((ROWS, HEADS * HEAD), jnp.bfloat16),
        in_specs=[SMEM] + [ANY] * len(parts) + [HBM] * len(before),
        out_specs=HBM,
        scratch_shapes=[pltpu.SemaphoreType.DMA((XS * sum(heads for _, heads in chunks),))],
        input_output_aliases={1 + len(parts): 0} if before else {},
        compiler_params=params(2),
    )(place, *parts, *before)


def joined(*values):
    return lax.optimization_barrier(values)


def per_device(queries, keys, values, latents, latent_owner, token_source, doc_lengths):
    outer = lax.axis_index("outer").astype(jnp.int32)
    inner = lax.axis_index("inner").astype(jnp.int32)
    z, x, core = inner >> 3, (inner >> 1) & 3, inner & 1
    place = jnp.stack([x, core, z, outer])
    kinds = latents.transpose(1, 0, 2)

    small = [(kind, h) for h in range(GROUP) for kind in (1, 2, 0)]
    keyed = [[(t, first + h) for h in range(heads) for t in ("k", "v")] for first, heads in CHUNKS]
    asked = [("q", h) for h in range(GROUP)]

    tensors = {"k": keys, "v": values, "latents": kinds, "sources": token_source.reshape(2, HEAD)}
    kv1, lat = pack(place, latent_owner, tensors, [keyed[0]], small)
    planned = plan(place, doc_lengths)
    lat = across_x(lat)
    lat[1], kv1 = joined(lat[1], kv1)

    near = jnp.stack(lat)
    near_z, far, kv1 = send(near, TO_Z), send(near, TO_CORE), across_x(kv1)
    kv2, q = pack(place, latent_owner, {"k": keys, "v": values, "q": queries}, [keyed[1], asked])
    near_z, far, kv1, kv2, q, planned = joined(near_z, far, kv1, kv2, q, planned)

    lat = near, near_z, far, send(near_z, TO_CORE)
    q = across_x(q)
    hot, keep = marks(place, lat)
    kind = {"q": 0, "k": 1, "v": 2}

    def merged(parts, slabs):
        return merge(parts, 0, lat, hot, keep, [(kind[t], 2 + small.index((kind[t], h))) for t, h in slabs])

    own1 = merged(kv1, keyed[0])
    before1 = send(own1, TO_NEXT)
    twin1 = send(own1, TO_CORE)
    q, twin1, kv2 = joined(q, twin1, kv2)

    kv2 = across_x(kv2)
    query = merged(q, asked)
    first, second = CHUNKS[0][1], CHUNKS[1][1]
    state = attend("own", planned, query, (own1, twin1), first)
    own2 = merged(kv2, keyed[1])
    before1, own2, state = joined(before1, own2, state)

    before2 = send(own2, TO_NEXT)
    sources = before1, send(before1, TO_CORE)
    done1 = attend("before", planned, query, sources, first, 0, 0, state)
    twin2 = send(own2, TO_CORE)
    out1 = across_x(done1)
    state = attend("own", planned, query, (own2, twin2), second, first)
    mixed = unpack(place, out1, CHUNKS[:1])
    before2, mixed, state = joined(before2, mixed, state)

    sources = before2, send(before2, TO_CORE)
    out2 = across_x(attend("before", planned, query, sources, second, first, 0, state))
    return unpack(place, out2, CHUNKS[1:], (mixed,))


def solution(mesh):
    return jax.shard_map(
        per_device,
        mesh=mesh,
        in_specs=(
            P(("outer", "inner"), None),
            P(("outer", "inner"), None),
            P(("outer", "inner"), None),
            P(("outer", "inner"), None, None),
            P(("outer", "inner")),
            P(("outer", "inner")),
            P(),
        ),
        out_specs=P(("outer", "inner"), None),
        check_vma=False,
    )
```

profile of v0, /device:TPU:9, one launch (start us, length us, event | category | flops | bytes accessed | tf_op | source)
XLA Modules:
  0.0 132.9 jit_solution(11342220390583093262)
XLA Ops:
  0.1 3.1 %shard_map.73 = (bf16[6,256,128]{2,1,0:T(8,128)(2,1)S(1)}, bf16[6,256,128]{2,1,0:T(8,128)(2,1)S(1)}, bf16[6,256,128]{2,1,0:T(8,128)(2,1)S(1)}, bf16[6,256,128]{2...) custom-call(s32[4]{0:T(128)S(1)} %pad_add_fusion.place, ...), custom_call_target="tpu_custom_call" | custom-call | tf_op jit(solution)/shard_map/pallas_call | solution.py:129
  3.2 2.5 %collective-permute-start = (bf16[17,32,128]{2,1,0:T(8,128)(2,1)S(1)}, bf16[17,32,128]{2,1,0:T(8,128)(2,1)S(1)}, u32[]{:S(2)}, u32[]{:S(2)}) collective-permute-start(bf16[17,32,128]{2,1,0:T(8,128)(2,1)S(1)} %get-tuple-element.80), channel_id=1, source_target_pairs={{0,6},{1,7},{2,0},{3,1},{4,2},{5,3},{6,4},{7,5},{8,14},{9,15},{10,... | collective-permute-start | bytes 417800 | tf_op jit(solution)/shard_map/ppermute | solution.py:44
  6.9 2.0 %collective-permute-done = bf16[17,32,128]{2,1,0:T(8,128)(2,1)S(1)} collective-permute-done((bf16[17,32,128]{2,1,0:T(8,128)(2,1)S(1)}, bf16[17,32,128]{2,1,0:T(8,128)(2,1)S(1)}, u32[]{:S(2)}, u32[]{:S(2)}) %collective-permute-start) | collective-permute-done | bytes 139296 | tf_op jit(solution)/shard_map/ppermute | solution.py:44
  8.9 2.6 %collective-permute-done.1 = bf16[17,32,128]{2,1,0:T(8,128)(2,1)S(1)} collective-permute-done((bf16[17,32,128]{2,1,0:T(8,128)(2,1)S(1)}, bf16[17,32,128]{2,1,0:T(8,128)(2,1)S(1)}, u32[]{:S(2)}, u32[]{:S(2)}) %collective-permute-start.1) | collective-permute-done | bytes 139296 | tf_op jit(solution)/shard_map/ppermute | solution.py:44
  11.5 4.3 %collective-permute-done.2 = bf16[17,32,128]{2,1,0:T(8,128)(2,1)S(1)} collective-permute-done((bf16[17,32,128]{2,1,0:T(8,128)(2,1)S(1)}, bf16[17,32,128]{2,1,0:T(8,128)(2,1)S(1)}, u32[]{:S(2)}, u32[]{:S(2)}) %collective-permute-start.2) | collective-permute-done | bytes 139296 | tf_op jit(solution)/shard_map/ppermute | solution.py:44
  15.8 1.7 %collective-permute-start.3 = (bf16[4,17,32,128]{3,2,1,0:T(8,128)(2,1)S(1)}, bf16[4,17,32,128]{3,2,1,0:T(8,128)(2,1)S(1)}, u32[]{:S(2)}, u32[]{:S(2)}) collective-permute-start(bf16[4,17,32,128]{3,2,1,0:T(8,128)(2,1)S(1)} %pad_maximum_fusion.near.refs_4_), channel_id=1, source_target_pairs={{0,8},{1,9},{2,10},{3,11},{4,12},{5,13},{6,14},{7,15},{8,0},{9,1},... | collective-permute-start | bytes 1671176 | tf_op jit(solution)/shard_map/ppermute | solution.py:44
  19.9 2.6 %shard_map.74 = (bf16[4,256,128]{2,1,0:T(8,128)(2,1)S(1)}, bf16[4,256,128]{2,1,0:T(8,128)(2,1)S(1)}, bf16[4,256,128]{2,1,0:T(8,128)(2,1)S(1)}, bf16[4,256,128]{2...) custom-call(s32[4]{0:T(128)S(1)} %pad_add_fusion.place, ...), custom_call_target="tpu_custom_call" | custom-call | tf_op jit(solution)/shard_map/pallas_call | solution.py:129
  22.5 2.6 %shard_map.75 = (s32[4,1,256]{2,1,0:T(1,128)S(1)}, s32[4,52]{1,0:T(4,128)S(1)}) custom-call(s32[4]{0:T(128)S(1)} %pad_add_fusion.place, s32[64]{0:T(128)S(1)} %copy-done), custom_call_target="tpu_custom_call" | custom-call | tf_op jit(solution)/shard_map/pallas_call | solution.py:268
  25.1 4.0 %collective-permute-done.5.refs_1_ = bf16[6,256,128]{2,1,0:T(8,128)(2,1)S(1)} collective-permute-done((bf16[6,256,128]{2,1,0:T(8,128)(2,1)S(1)}, bf16[6,256,128]{2,1,0:T(8,128)(2,1)S(1)}, u32[]{:S(2)}, u32[]{:S(2)}) %collective-permute-start.5) | collective-permute-done | bytes 393248 | tf_op jit(solution)/shard_map/ppermute | solution.py:44
  29.1 1.5 %collective-permute-done.6.refs_2_ = bf16[6,256,128]{2,1,0:T(8,128)(2,1)S(1)} collective-permute-done((bf16[6,256,128]{2,1,0:T(8,128)(2,1)S(1)}, bf16[6,256,128]{2,1,0:T(8,128)(2,1)S(1)}, u32[]{:S(2)}, u32[]{:S(2)}) %collective-permute-start.6) | collective-permute-done | bytes 393248 | tf_op jit(solution)/shard_map/ppermute | solution.py:44
  30.7 9.0 %collective-permute-done.7.refs_3_ = bf16[6,256,128]{2,1,0:T(8,128)(2,1)S(1)} collective-permute-done((bf16[6,256,128]{2,1,0:T(8,128)(2,1)S(1)}, bf16[6,256,128]{2,1,0:T(8,128)(2,1)S(1)}, u32[]{:S(2)}, u32[]{:S(2)}) %collective-permute-start.7) | collective-permute-done | bytes 393248 | tf_op jit(solution)/shard_map/ppermute | solution.py:44
  40.2 1.6 %collective-permute-done.11.far_z.refs_7_ = bf16[4,17,32,128]{3,2,1,0:T(8,128)(2,1)S(1)} collective-permute-done((bf16[4,17,32,128]{3,2,1,0:T(8,128)(2,1)S(1)}, bf16[4,17,32,128]{3,2,1,0:T(8,128)(2,1)S(1)}, u32[]{:S(2)}, u32[]{:S(2)}) %collective-permute-start.11) | collective-permute-done | bytes 557088 | tf_op jit(solution)/shard_map/ppermute | solution.py:44
  42.6 2.3 %shard_map.77.refs_0_ = bf16[4,6,256,128]{3,2,1,0:T(8,128)(2,1)S(1)} custom-call(bf16[6,256,128]{2,1,0:T(8,128)(2,1)S(1)} %get-tuple-element.108.refs_0_, bf16[6,256,128]{2,1,0:T(8,128)(2,1)S(1)} %collective-permute-done.5.refs_1_, bf16[6,256,128]{2,1,0:T(8,128)(2,1)S(1)} %collective-permute-done.6.refs_2_, ...), custom_call_target="tpu_custom_call" | custom-call | tf_op jit(solution)/shard_map/pallas_call | solution.py:197
  45.4 1.9 %collective-permute-start.13 = (bf16[4,6,256,128]{3,2,1,0:T(8,128)(2,1)S(1)}, bf16[4,6,256,128]{3,2,1,0:T(8,128)(2,1)S(1)}, u32[]{:S(2)}, u32[]{:S(2)}) collective-permute-start(bf16[4,6,256,128]{3,2,1,0:T(8,128)(2,1)S(1)} %shard_map.77.refs_0_), channel_id=1, source_target_pairs={{0,8},{1,9},{2,10},{3,11},{4,12},{5,13},{6,14},{7,15},{8,16},{9,17... | collective-permute-start | bytes 4718600 | tf_op jit(solution)/shard_map/ppermute | solution.py:44
  47.3 2.7 %collective-permute-start.8 = (bf16[5,256,128]{2,1,0:T(8,128)(2,1)S(1)}, bf16[5,256,128]{2,1,0:T(8,128)(2,1)S(1)}, u32[]{:S(2)}, u32[]{:S(2)}) collective-permute-start(bf16[5,256,128]{2,1,0:T(8,128)(2,1)S(1)} %get-tuple-element.105), channel_id=1, source_target_pairs={{0,6},{1,7},{2,0},{3,1},{4,2},{5,3},{6,4},{7,5},{8,14},{9,15},{10,... | collective-permute-start | bytes 983048 | tf_op jit(solution)/shard_map/ppermute | solution.py:44
  50.0 14.6 %collective-permute-done.10.refs_3_ = bf16[5,256,128]{2,1,0:T(8,128)(2,1)S(1)} collective-permute-done((bf16[5,256,128]{2,1,0:T(8,128)(2,1)S(1)}, bf16[5,256,128]{2,1,0:T(8,128)(2,1)S(1)}, u32[]{:S(2)}, u32[]{:S(2)}) %collective-permute-start.10) | collective-permute-done | bytes 327712 | tf_op jit(solution)/shard_map/ppermute | solution.py:44
  64.6 2.4 %collective-permute-start.14 = (bf16[4,256,128]{2,1,0:T(8,128)(2,1)S(1)}, bf16[4,256,128]{2,1,0:T(8,128)(2,1)S(1)}, u32[]{:S(2)}, u32[]{:S(2)}) collective-permute-start(bf16[4,256,128]{2,1,0:T(8,128)(2,1)S(1)} %get-tuple-element.125), channel_id=1, source_target_pairs={{0,6},{1,7},{2,0},{3,1},{4,2},{5,3},{6,4},{7,5},{8,14},{9,15},{10,... | collective-permute-start | bytes 786440 | tf_op jit(solution)/shard_map/ppermute | solution.py:44
  67.7 1.8 %shard_map.78.q_hbm = bf16[4,5,256,128]{3,2,1,0:T(8,128)(2,1)S(1)} custom-call(bf16[5,256,128]{2,1,0:T(8,128)(2,1)S(1)} %get-tuple-element.120.refs_0_, bf16[5,256,128]{2,1,0:T(8,128)(2,1)S(1)} %collective-permute-done.8.refs_1_, bf16[5,256,128]{2,1,0:T(8,128)(2,1)S(1)} %collective-permute-done.9.refs_2_, ...), custom_call_target="tpu_custom_call" | custom-call | tf_op jit(solution)/shard_map/pallas_call | solution.py:197
  69.5 9.2 %shard_map.80 = (f32[3,4,8,256]{3,2,1,0:T(8,128)S(1)}, f32[3,4,8,256]{3,2,1,0:T(8,128)S(1)}, f32[3,4,128,256]{3,2,1,0:T(8,128)S(1)}) custom-call(s32[4,52]{1,0:T(4,128)S(1)} %get-tuple-element.102.items, s32[4,1,256]{2,1,0:T(1,128)S(1)} %get-tuple-element.103.begins, bf16[4,5,256,128]{3,2,1,0:T(8,128)(2,1)S(1)} %shard_map.78.q_hbm, ...), custom_call_target="tpu_custom_call" | custom-call | tf_op jit(solution)/shard_map/pallas_call | solution.py:370
  78.7 3.0 %collective-permute-done.16.refs_3_ = bf16[4,256,128]{2,1,0:T(8,128)(2,1)S(1)} collective-permute-done((bf16[4,256,128]{2,1,0:T(8,128)(2,1)S(1)}, bf16[4,256,128]{2,1,0:T(8,128)(2,1)S(1)}, u32[]{:S(2)}, u32[]{:S(2)}) %collective-permute-start.16) | collective-permute-done | bytes 262176 | tf_op jit(solution)/shard_map/ppermute | solution.py:44
  84.9 3.2 %collective-permute-start.17 = (bf16[4,4,256,128]{3,2,1,0:T(8,128)(2,1)S(1)}, bf16[4,4,256,128]{3,2,1,0:T(8,128)(2,1)S(1)}, u32[]{:S(2)}, u32[]{:S(2)}) collective-permute-start(bf16[4,4,256,128]{3,2,1,0:T(8,128)(2,1)S(1)} %shard_map.79.refs_0_), channel_id=1, source_target_pairs={{0,8},{1,9},{2,10},{3,11},{4,12},{5,13},{6,14},{7,15},{8,16},{9,17... | collective-permute-start | bytes 3145736 | tf_op jit(solution)/shard_map/ppermute | solution.py:44
  88.2 7.5 %shard_map.81 = (bf16[3,256,128]{2,1,0:T(8,128)(2,1)S(1)}, bf16[3,256,128]{2,1,0:T(8,128)(2,1)S(1)}, bf16[3,256,128]{2,1,0:T(8,128)(2,1)S(1)}, bf16[3,256,128]{2,1,0:T(8,128)(2,1)S(1)}) custom-call(s32[4,52]{1,0:T(4,128)S(1)} %get-tuple-element.102.items, s32[4,1,256]{2,1,0:T(1,128)S(1)} %get-tuple-element.103.begins, ...), custom_call_target="tpu_custom_call" | custom-call | tf_op jit(solution)/shard_map/pallas_call | solution.py:370
  96.5 1.7 %collective-permute-start.20 = (bf16[3,256,128]{2,1,0:T(8,128)(2,1)S(1)}, bf16[3,256,128]{2,1,0:T(8,128)(2,1)S(1)}, u32[]{:S(2)}, u32[]{:S(2)}) collective-permute-start(bf16[3,256,128]{2,1,0:T(8,128)(2,1)S(1)} %get-tuple-element.139), channel_id=1, source_target_pairs={{0,4},{1,5},{2,6},{3,7},{4,0},{5,1},{6,2},{7,3},{8,12},{9,13},{10,... | collective-permute-start | bytes 589832 | tf_op jit(solution)/shard_map/ppermute | solution.py:44
  98.1 6.2 %shard_map.83 = (f32[2,4,8,256]{3,2,1,0:T(8,128)S(1)}, f32[2,4,8,256]{3,2,1,0:T(8,128)S(1)}, f32[2,4,128,256]{3,2,1,0:T(8,128)S(1)}) custom-call(s32[4,52]{1,0:T(4,128)S(1)} %get-tuple-element.102.items, s32[4,1,256]{2,1,0:T(1,128)S(1)} %get-tuple-element.103.begins, bf16[4,5,256,128]{3,2,1,0:T(8,128)(2,1)S(1)} %shard_map.78.q_hbm, ...), custom_call_target="tpu_custom_call" | custom-call | tf_op jit(solution)/shard_map/pallas_call | solution.py:370
  104.4 4.5 %collective-permute-done.21.refs_3_ = bf16[3,256,128]{2,1,0:T(8,128)(2,1)S(1)} collective-permute-done((bf16[3,256,128]{2,1,0:T(8,128)(2,1)S(1)}, bf16[3,256,128]{2,1,0:T(8,128)(2,1)S(1)}, u32[]{:S(2)}, u32[]{:S(2)}) %collective-permute-start.21) | collective-permute-done | bytes 196640 | tf_op jit(solution)/shard_map/ppermute | solution.py:44
  108.9 1.5 %shard_map.82.refs_4_ = bf16[256,2560]{1,0:T(8,128)(2,1)} custom-call(s32[4]{0:T(128)S(1)} %pad_add_fusion.place, bf16[3,256,128]{2,1,0:T(8,128)(2,1)S(1)} %get-tuple-element.137.refs_0_, bf16[3,256,128]{2,1,0:T(8,128)(2,1)S(1)} %collective-permute-done.19.refs_1_, bf16[3,256,128]{2,1,0:T(8,128)(2,1)S(1)} %collective-permute-done.20.refs_2_, ...), custom_call_target="tpu_custom_call" | custom-call | tf_op jit(solution)/shard_map/pallas_call | solution.py:400
  110.4 1.5 %collective-permute-done.17.refs_0_ = bf16[4,4,256,128]{3,2,1,0:T(8,128)(2,1)S(1)} collective-permute-done((bf16[4,4,256,128]{3,2,1,0:T(8,128)(2,1)S(1)}, bf16[4,4,256,128]{3,2,1,0:T(8,128)(2,1)S(1)}, u32[]{:S(2)}, u32[]{:S(2)}) %collective-permute-start.17) | collective-permute-done | bytes 1048608 | tf_op jit(solution)/shard_map/ppermute | solution.py:44
  113.3 2.3 %collective-permute-done.23.refs_1_ = bf16[4,4,256,128]{3,2,1,0:T(8,128)(2,1)S(1)} collective-permute-done((bf16[4,4,256,128]{3,2,1,0:T(8,128)(2,1)S(1)}, bf16[4,4,256,128]{3,2,1,0:T(8,128)(2,1)S(1)}, u32[]{:S(2)}, u32[]{:S(2)}) %collective-permute-start.23) | collective-permute-done | bytes 1048608 | tf_op jit(solution)/shard_map/ppermute | solution.py:44
  115.6 5.2 %shard_map.84 = (bf16[2,256,128]{2,1,0:T(8,128)(2,1)S(1)}, bf16[2,256,128]{2,1,0:T(8,128)(2,1)S(1)}, bf16[2,256,128]{2,1,0:T(8,128)(2,1)S(1)}, bf16[2,256,128]{2,1,0:T(8,128)(2,1)S(1)}) custom-call(s32[4,52]{1,0:T(4,128)S(1)} %get-tuple-element.102.items, s32[4,1,256]{2,1,0:T(1,128)S(1)} %get-tuple-element.103.begins, ...), custom_call_target="tpu_custom_call" | custom-call | tf_op jit(solution)/shard_map/pallas_call | solution.py:370
  122.4 3.2 %collective-permute-done.24.refs_1_ = bf16[2,256,128]{2,1,0:T(8,128)(2,1)S(1)} collective-permute-done((bf16[2,256,128]{2,1,0:T(8,128)(2,1)S(1)}, bf16[2,256,128]{2,1,0:T(8,128)(2,1)S(1)}, u32[]{:S(2)}, u32[]{:S(2)}) %collective-permute-start.24) | collective-permute-done | bytes 131104 | tf_op jit(solution)/shard_map/ppermute | solution.py:44
  125.6 1.9 %collective-permute-done.25.refs_2_ = bf16[2,256,128]{2,1,0:T(8,128)(2,1)S(1)} collective-permute-done((bf16[2,256,128]{2,1,0:T(8,128)(2,1)S(1)}, bf16[2,256,128]{2,1,0:T(8,128)(2,1)S(1)}, u32[]{:S(2)}, u32[]{:S(2)}) %collective-permute-start.25) | collective-permute-done | bytes 131104 | tf_op jit(solution)/shard_map/ppermute | solution.py:44
  127.5 3.8 %collective-permute-done.26.refs_3_ = bf16[2,256,128]{2,1,0:T(8,128)(2,1)S(1)} collective-permute-done((bf16[2,256,128]{2,1,0:T(8,128)(2,1)S(1)}, bf16[2,256,128]{2,1,0:T(8,128)(2,1)S(1)}, u32[]{:S(2)}, u32[]{:S(2)}) %collective-permute-start.26) | collective-permute-done | bytes 131104 | tf_op jit(solution)/shard_map/ppermute | solution.py:44
  (39 shorter events, 14.4 us)
Async XLA Ops:
  3.2 5.7 %collective-permute-start = (bf16[17,32,128]{2,1,0:T(8,128)(2,1)S(1)}, bf16[17,32,128]{2,1,0:T(8,128)(2,1)S(1)}, u32[]{:S(2)}, u32[]{:S(2)}) collective-permute-start(bf16[17,32,128]{2,1,0:T(8,128)(2,1)S(1)} %get-tuple-element.80), channel_id=1, source_target_pairs={{0,6},{1,7},{2,0},{3,1},{4,2},{5,3},{6,4},{7,5},{8,14},{9,15},{10,... | collective-permute-start | bytes 417800 | tf_op jit(solution)/shard_map/ppermute | solution.py:44
  5.7 5.7 %collective-permute-start.1 = (bf16[17,32,128]{2,1,0:T(8,128)(2,1)S(1)}, bf16[17,32,128]{2,1,0:T(8,128)(2,1)S(1)}, u32[]{:S(2)}, u32[]{:S(2)}) collective-permute-start(bf16[17,32,128]{2,1,0:T(8,128)(2,1)S(1)} %get-tuple-element.86), channel_id=1, source_target_pairs={{0,4},{1,5},{2,6},{3,7},{4,0},{5,1},{6,2},{7,3},{8,12},{9,13},{10,... | collective-permute-start | bytes 417800 | tf_op jit(solution)/shard_map/ppermute | solution.py:44
  6.3 9.5 %collective-permute-start.2 = (bf16[17,32,128]{2,1,0:T(8,128)(2,1)S(1)}, bf16[17,32,128]{2,1,0:T(8,128)(2,1)S(1)}, u32[]{:S(2)}, u32[]{:S(2)}) collective-permute-start(bf16[17,32,128]{2,1,0:T(8,128)(2,1)S(1)} %get-tuple-element.87), channel_id=1, source_target_pairs={{0,2},{1,3},{2,4},{3,5},{4,6},{5,7},{6,0},{7,1},{8,10},{9,11},{10,... | collective-permute-start | bytes 417800 | tf_op jit(solution)/shard_map/ppermute | solution.py:44
  15.8 6.7 %copy-start = (s32[64]{0:T(128)S(1)}, s32[64]{0:T(128)}, u32[]{:S(2)}) copy-start(s32[64]{0:T(128)} %lengths.1) | copy-start | bytes 772
  15.8 23.9 %collective-permute-start.3 = (bf16[4,17,32,128]{3,2,1,0:T(8,128)(2,1)S(1)}, bf16[4,17,32,128]{3,2,1,0:T(8,128)(2,1)S(1)}, u32[]{:S(2)}, u32[]{:S(2)}) collective-permute-start(bf16[4,17,32,128]{3,2,1,0:T(8,128)(2,1)S(1)} %pad_maximum_fusion.near.refs_4_), channel_id=1, source_target_pairs={{0,8},{1,9},{2,10},{3,11},{4,12},{5,13},{6,14},{7,15},{8,0},{9,1},... | collective-permute-start | bytes 1671176 | tf_op jit(solution)/shard_map/ppermute | solution.py:44
  17.5 22.2 %collective-permute-start.4 = (bf16[4,17,32,128]{3,2,1,0:T(8,128)(2,1)S(1)}, bf16[4,17,32,128]{3,2,1,0:T(8,128)(2,1)S(1)}, u32[]{:S(2)}, u32[]{:S(2)}) collective-permute-start(bf16[4,17,32,128]{3,2,1,0:T(8,128)(2,1)S(1)} %pad_maximum_fusion.near.refs_4_), channel_id=1, source_target_pairs={{0,1},{1,0},{2,3},{3,2},{4,5},{5,4},{6,7},{7,6},{8,9},{9,8},{10,11... | collective-permute-start | bytes 1671176 | tf_op jit(solution)/shard_map/ppermute | solution.py:44
  18.4 10.7 %collective-permute-start.5 = (bf16[6,256,128]{2,1,0:T(8,128)(2,1)S(1)}, bf16[6,256,128]{2,1,0:T(8,128)(2,1)S(1)}, u32[]{:S(2)}, u32[]{:S(2)}) collective-permute-start(bf16[6,256,128]{2,1,0:T(8,128)(2,1)S(1)} %get-tuple-element.89), channel_id=1, source_target_pairs={{0,6},{1,7},{2,0},{3,1},{4,2},{5,3},{6,4},{7,5},{8,14},{9,15},{10,... | collective-permute-start | bytes 1179656 | tf_op jit(solution)/shard_map/ppermute | solution.py:44
  18.7 12.0 %collective-permute-start.6 = (bf16[6,256,128]{2,1,0:T(8,128)(2,1)S(1)}, bf16[6,256,128]{2,1,0:T(8,128)(2,1)S(1)}, u32[]{:S(2)}, u32[]{:S(2)}) collective-permute-start(bf16[6,256,128]{2,1,0:T(8,128)(2,1)S(1)} %get-tuple-element.90), channel_id=1, source_target_pairs={{0,4},{1,5},{2,6},{3,7},{4,0},{5,1},{6,2},{7,3},{8,12},{9,13},{10,... | collective-permute-start | bytes 1179656 | tf_op jit(solution)/shard_map/ppermute | solution.py:44
  19.2 20.5 %collective-permute-start.7 = (bf16[6,256,128]{2,1,0:T(8,128)(2,1)S(1)}, bf16[6,256,128]{2,1,0:T(8,128)(2,1)S(1)}, u32[]{:S(2)}, u32[]{:S(2)}) collective-permute-start(bf16[6,256,128]{2,1,0:T(8,128)(2,1)S(1)} %get-tuple-element.91), channel_id=1, source_target_pairs={{0,2},{1,3},{2,4},{3,5},{4,6},{5,7},{6,0},{7,1},{8,10},{9,11},{10,... | collective-permute-start | bytes 1179656 | tf_op jit(solution)/shard_map/ppermute | solution.py:44
  39.7 2.1 %collective-permute-start.11 = (bf16[4,17,32,128]{3,2,1,0:T(8,128)(2,1)S(1)}, bf16[4,17,32,128]{3,2,1,0:T(8,128)(2,1)S(1)}, u32[]{:S(2)}, u32[]{:S(2)}) collective-permute-start(bf16[4,17,32,128]{3,2,1,0:T(8,128)(2,1)S(1)} %collective-permute-done.3.near_z.refs_5_), channel_id=1, source_target_pairs={{0,1},{1,0},{2,3},{3,2},{4,5},{5,4},{6,7},{7,6},{8,9},{9,8},{10,11... | collective-permute-start | bytes 1671176 | tf_op jit(solution)/shard_map/ppermute | solution.py:44
  44.9 19.7 %collective-permute-start.12 = (bf16[4,6,256,128]{3,2,1,0:T(8,128)(2,1)S(1)}, bf16[4,6,256,128]{3,2,1,0:T(8,128)(2,1)S(1)}, u32[]{:S(2)}, u32[]{:S(2)}) collective-permute-start(bf16[4,6,256,128]{3,2,1,0:T(8,128)(2,1)S(1)} %shard_map.77.refs_0_), channel_id=1, source_target_pairs={{0,1},{1,0},{2,3},{3,2},{4,5},{5,4},{6,7},{7,6},{8,9},{9,8},{10,11... | collective-permute-start | bytes 4718600 | tf_op jit(solution)/shard_map/ppermute | solution.py:44
  45.4 38.6 %collective-permute-start.13 = (bf16[4,6,256,128]{3,2,1,0:T(8,128)(2,1)S(1)}, bf16[4,6,256,128]{3,2,1,0:T(8,128)(2,1)S(1)}, u32[]{:S(2)}, u32[]{:S(2)}) collective-permute-start(bf16[4,6,256,128]{3,2,1,0:T(8,128)(2,1)S(1)} %shard_map.77.refs_0_), channel_id=1, source_target_pairs={{0,8},{1,9},{2,10},{3,11},{4,12},{5,13},{6,14},{7,15},{8,16},{9,17... | collective-permute-start | bytes 4718600 | tf_op jit(solution)/shard_map/ppermute | solution.py:44
  47.3 17.4 %collective-permute-start.10 = (bf16[5,256,128]{2,1,0:T(8,128)(2,1)S(1)}, bf16[5,256,128]{2,1,0:T(8,128)(2,1)S(1)}, u32[]{:S(2)}, u32[]{:S(2)}) collective-permute-start(bf16[5,256,128]{2,1,0:T(8,128)(2,1)S(1)} %get-tuple-element.107), channel_id=1, source_target_pairs={{0,2},{1,3},{2,4},{3,5},{4,6},{5,7},{6,0},{7,1},{8,10},{9,11},{10,... | collective-permute-start | bytes 983048 | tf_op jit(solution)/shard_map/ppermute | solution.py:44
  47.3 17.3 %collective-permute-start.8 = (bf16[5,256,128]{2,1,0:T(8,128)(2,1)S(1)}, bf16[5,256,128]{2,1,0:T(8,128)(2,1)S(1)}, u32[]{:S(2)}, u32[]{:S(2)}) collective-permute-start(bf16[5,256,128]{2,1,0:T(8,128)(2,1)S(1)} %get-tuple-element.105), channel_id=1, source_target_pairs={{0,6},{1,7},{2,0},{3,1},{4,2},{5,3},{6,4},{7,5},{8,14},{9,15},{10,... | collective-permute-start | bytes 983048 | tf_op jit(solution)/shard_map/ppermute | solution.py:44
  50.0 14.6 %collective-permute-start.9 = (bf16[5,256,128]{2,1,0:T(8,128)(2,1)S(1)}, bf16[5,256,128]{2,1,0:T(8,128)(2,1)S(1)}, u32[]{:S(2)}, u32[]{:S(2)}) collective-permute-start(bf16[5,256,128]{2,1,0:T(8,128)(2,1)S(1)} %get-tuple-element.106), channel_id=1, source_target_pairs={{0,4},{1,5},{2,6},{3,7},{4,0},{5,1},{6,2},{7,3},{8,12},{9,13},{10,... | collective-permute-start | bytes 983048 | tf_op jit(solution)/shard_map/ppermute | solution.py:44
  64.6 14.0 %collective-permute-start.14 = (bf16[4,256,128]{2,1,0:T(8,128)(2,1)S(1)}, bf16[4,256,128]{2,1,0:T(8,128)(2,1)S(1)}, u32[]{:S(2)}, u32[]{:S(2)}) collective-permute-start(bf16[4,256,128]{2,1,0:T(8,128)(2,1)S(1)} %get-tuple-element.125), channel_id=1, source_target_pairs={{0,6},{1,7},{2,0},{3,1},{4,2},{5,3},{6,4},{7,5},{8,14},{9,15},{10,... | collective-permute-start | bytes 786440 | tf_op jit(solution)/shard_map/ppermute | solution.py:44
  67.0 11.7 %collective-permute-start.15 = (bf16[4,256,128]{2,1,0:T(8,128)(2,1)S(1)}, bf16[4,256,128]{2,1,0:T(8,128)(2,1)S(1)}, u32[]{:S(2)}, u32[]{:S(2)}) collective-permute-start(bf16[4,256,128]{2,1,0:T(8,128)(2,1)S(1)} %get-tuple-element.126), channel_id=1, source_target_pairs={{0,4},{1,5},{2,6},{3,7},{4,0},{5,1},{6,2},{7,3},{8,12},{9,13},{10,... | collective-permute-start | bytes 786440 | tf_op jit(solution)/shard_map/ppermute | solution.py:44
  67.0 14.7 %collective-permute-start.16 = (bf16[4,256,128]{2,1,0:T(8,128)(2,1)S(1)}, bf16[4,256,128]{2,1,0:T(8,128)(2,1)S(1)}, u32[]{:S(2)}, u32[]{:S(2)}) collective-permute-start(bf16[4,256,128]{2,1,0:T(8,128)(2,1)S(1)} %get-tuple-element.127), channel_id=1, source_target_pairs={{0,2},{1,3},{2,4},{3,5},{4,6},{5,7},{6,0},{7,1},{8,10},{9,11},{10,... | collective-permute-start | bytes 786440 | tf_op jit(solution)/shard_map/ppermute | solution.py:44
  84.0 4.2 %collective-permute-start.18 = (bf16[4,6,256,128]{3,2,1,0:T(8,128)(2,1)S(1)}, bf16[4,6,256,128]{3,2,1,0:T(8,128)(2,1)S(1)}, u32[]{:S(2)}, u32[]{:S(2)}) collective-permute-start(bf16[4,6,256,128]{3,2,1,0:T(8,128)(2,1)S(1)} %collective-permute-done.13.refs_0_), channel_id=1, source_target_pairs={{0,1},{1,0},{2,3},{3,2},{4,5},{5,4},{6,7},{7,6},{8,9},{9,8},{10,11... | collective-permute-start | bytes 4718600 | tf_op jit(solution)/shard_map/ppermute | solution.py:44
  84.9 13.2 %collective-permute-start.22 = (bf16[4,4,256,128]{3,2,1,0:T(8,128)(2,1)S(1)}, bf16[4,4,256,128]{3,2,1,0:T(8,128)(2,1)S(1)}, u32[]{:S(2)}, u32[]{:S(2)}) collective-permute-start(bf16[4,4,256,128]{3,2,1,0:T(8,128)(2,1)S(1)} %shard_map.79.refs_0_), channel_id=1, source_target_pairs={{0,1},{1,0},{2,3},{3,2},{4,5},{5,4},{6,7},{7,6},{8,9},{9,8},{10,11... | collective-permute-start | bytes 3145736 | tf_op jit(solution)/shard_map/ppermute | solution.py:44
  84.9 27.0 %collective-permute-start.17 = (bf16[4,4,256,128]{3,2,1,0:T(8,128)(2,1)S(1)}, bf16[4,4,256,128]{3,2,1,0:T(8,128)(2,1)S(1)}, u32[]{:S(2)}, u32[]{:S(2)}) collective-permute-start(bf16[4,4,256,128]{3,2,1,0:T(8,128)(2,1)S(1)} %shard_map.79.refs_0_), channel_id=1, source_target_pairs={{0,8},{1,9},{2,10},{3,11},{4,12},{5,13},{6,14},{7,15},{8,16},{9,17... | collective-permute-start | bytes 3145736 | tf_op jit(solution)/shard_map/ppermute | solution.py:44
  95.8 8.6 %collective-permute-start.19 = (bf16[3,256,128]{2,1,0:T(8,128)(2,1)S(1)}, bf16[3,256,128]{2,1,0:T(8,128)(2,1)S(1)}, u32[]{:S(2)}, u32[]{:S(2)}) collective-permute-start(bf16[3,256,128]{2,1,0:T(8,128)(2,1)S(1)} %get-tuple-element.138), channel_id=1, source_target_pairs={{0,6},{1,7},{2,0},{3,1},{4,2},{5,3},{6,4},{7,5},{8,14},{9,15},{10,... | collective-permute-start | bytes 589832 | tf_op jit(solution)/shard_map/ppermute | solution.py:44
  96.5 7.9 %collective-permute-start.20 = (bf16[3,256,128]{2,1,0:T(8,128)(2,1)S(1)}, bf16[3,256,128]{2,1,0:T(8,128)(2,1)S(1)}, u32[]{:S(2)}, u32[]{:S(2)}) collective-permute-start(bf16[3,256,128]{2,1,0:T(8,128)(2,1)S(1)} %get-tuple-element.139), channel_id=1, source_target_pairs={{0,4},{1,5},{2,6},{3,7},{4,0},{5,1},{6,2},{7,3},{8,12},{9,13},{10,... | collective-permute-start | bytes 589832 | tf_op jit(solution)/shard_map/ppermute | solution.py:44
  98.1 10.8 %collective-permute-start.21 = (bf16[3,256,128]{2,1,0:T(8,128)(2,1)S(1)}, bf16[3,256,128]{2,1,0:T(8,128)(2,1)S(1)}, u32[]{:S(2)}, u32[]{:S(2)}) collective-permute-start(bf16[3,256,128]{2,1,0:T(8,128)(2,1)S(1)} %get-tuple-element.140), channel_id=1, source_target_pairs={{0,2},{1,3},{2,4},{3,5},{4,6},{5,7},{6,0},{7,1},{8,10},{9,11},{10,... | collective-permute-start | bytes 589832 | tf_op jit(solution)/shard_map/ppermute | solution.py:44
  111.9 3.6 %collective-permute-start.23 = (bf16[4,4,256,128]{3,2,1,0:T(8,128)(2,1)S(1)}, bf16[4,4,256,128]{3,2,1,0:T(8,128)(2,1)S(1)}, u32[]{:S(2)}, u32[]{:S(2)}) collective-permute-start(bf16[4,4,256,128]{3,2,1,0:T(8,128)(2,1)S(1)} %collective-permute-done.17.refs_0_), channel_id=1, source_target_pairs={{0,1},{1,0},{2,3},{3,2},{4,5},{5,4},{6,7},{7,6},{8,9},{9,8},{10,11... | collective-permute-start | bytes 3145736 | tf_op jit(solution)/shard_map/ppermute | solution.py:44
  120.8 4.8 %collective-permute-start.24 = (bf16[2,256,128]{2,1,0:T(8,128)(2,1)S(1)}, bf16[2,256,128]{2,1,0:T(8,128)(2,1)S(1)}, u32[]{:S(2)}, u32[]{:S(2)}) collective-permute-start(bf16[2,256,128]{2,1,0:T(8,128)(2,1)S(1)} %get-tuple-element.149), channel_id=1, source_target_pairs={{0,6},{1,7},{2,0},{3,1},{4,2},{5,3},{6,4},{7,5},{8,14},{9,15},{10,... | collective-permute-start | bytes 393224 | tf_op jit(solution)/shard_map/ppermute | solution.py:44
  121.6 5.9 %collective-permute-start.25 = (bf16[2,256,128]{2,1,0:T(8,128)(2,1)S(1)}, bf16[2,256,128]{2,1,0:T(8,128)(2,1)S(1)}, u32[]{:S(2)}, u32[]{:S(2)}) collective-permute-start(bf16[2,256,128]{2,1,0:T(8,128)(2,1)S(1)} %get-tuple-element.150), channel_id=1, source_target_pairs={{0,4},{1,5},{2,6},{3,7},{4,0},{5,1},{6,2},{7,3},{8,12},{9,13},{10,... | collective-permute-start | bytes 393224 | tf_op jit(solution)/shard_map/ppermute | solution.py:44
  122.1 9.2 %collective-permute-start.26 = (bf16[2,256,128]{2,1,0:T(8,128)(2,1)S(1)}, bf16[2,256,128]{2,1,0:T(8,128)(2,1)S(1)}, u32[]{:S(2)}, u32[]{:S(2)}) collective-permute-start(bf16[2,256,128]{2,1,0:T(8,128)(2,1)S(1)} %get-tuple-element.151), channel_id=1, source_target_pairs={{0,2},{1,3},{2,4},{3,5},{4,6},{5,7},{6,0},{7,1},{8,10},{9,11},{10,... | collective-permute-start | bytes 393224 | tf_op jit(solution)/shard_map/ppermute | solution.py:44
where the time goes:
time: 133 us
  waiting for transfers between devices  61 us (46%)
  Pallas kernels  45.6 us (34%)
  starting transfers between devices  25.8 us (19%)
    ppermute x27, waiting for transfers between devices, send(): return lax.ppermute(value, AXES, route)  61 us
    pallas_call x4, Pallas kernels, attend(): pl.pallas_call(functools.partial(attend_kernel, part, query_at, 2 * head_...  28.1 us
    ppermute x27, starting transfers between devices, send(): return lax.ppermute(value, AXES, route)  25.8 us
    pallas_call x2, Pallas kernels, pack(): pl.pallas_call(functools.partial(pack_kernel, parcels, small, order), out...  5.67 us
    pallas_call x3, Pallas kernels, merge(): pl.pallas_call(functools.partial(merge_kernel, base, work), out_shape=jax...  5.35 us
    pallas_call x2, Pallas kernels, unpack(): pl.pallas_call(functools.partial(unpack_kernel, chunks), out_shape=jax.Sh...  2.91 us
  transfers between devices with their start and end apart: 27, of which 16 were waited for; matrix products, arithmetic and copies ran while one was open for 0% of the time, Pallas kernels for 25%

commit v1 on v0

--- a/solution.py
+++ b/solution.py
@@ -423,8 +423,9 @@
     keyed = [[(t, first + h) for h in range(heads) for t in ("k", "v")] for first, heads in CHUNKS]
     asked = [("q", h) for h in range(GROUP)]
 
-    tensors = {"k": keys, "v": values, "latents": kinds, "sources": token_source.reshape(2, HEAD)}
-    kv1, lat = pack(place, latent_owner, tensors, [keyed[0]], small)
+    tensors = {"latents": kinds, "sources": token_source.reshape(2, HEAD)}
+    (lat,) = pack(place, latent_owner, tensors, [], small)
+    (kv1,) = pack(place, latent_owner, {"k": keys, "v": values}, [keyed[0]])
     planned = plan(place, doc_lengths)
     lat = across_x(lat)
     lat[1], kv1 = joined(lat[1], kv1)

time: 133 us -> 131 us (0.985)
  the two profiles are of different devices: /device:TPU:9 before, /device:TPU:32 now
where the time goes in v1:
time: 131 us
  waiting for transfers between devices  54.6 us (42%)
  Pallas kernels  46.8 us (36%)
  starting transfers between devices  28.6 us (22%)
    ppermute x27, waiting for transfers between devices, send(): return lax.ppermute(value, AXES, route)  54.6 us
    ppermute x27, starting transfers between devices, send(): return lax.ppermute(value, AXES, route)  28.6 us
    pallas_call x4, Pallas kernels, attend(): pl.pallas_call(functools.partial(attend_kernel, part, query_at, 2 * head_...  28.1 us
    pallas_call x3, Pallas kernels, pack(): pl.pallas_call(functools.partial(pack_kernel, parcels, small, order), out...  6.96 us
    pallas_call x3, Pallas kernels, merge(): pl.pallas_call(functools.partial(merge_kernel, base, work), out_shape=jax...  5.35 us
    pallas_call x2, Pallas kernels, unpack(): pl.pallas_call(functools.partial(unpack_kernel, chunks), out_shape=jax.Sh...  2.91 us
  transfers between devices with their start and end apart: 27, of which 16 were waited for; matrix products, arithmetic and copies ran while one was open for 0% of the time, Pallas kernels for 27%

profile of v1, /device:TPU:32, one launch (start us, length us, event | category | flops | bytes accessed | tf_op | source)
XLA Modules:
  0.0 130.5 jit_solution(18051181031539514721)
XLA Ops:
  0.1 2.2 %shard_map.73 = (bf16[17,32,128]{2,1,0:T(8,128)(2,1)S(1)}, bf16[17,32,128]{2,1,0:T(8,128)(2,1)S(1)}, bf16[17,32,128]{2,1,0:T(8,128)(2,1)S(1)}, bf16[17,32,128]{2,1,0:T(8,128)(2,1)S(1)}) custom-call(s32[4]{0:T(128)S(1)} %pad_add_fusion.place, s32[8]{0:T(128)} %owner.5, bf16[3,32,2560]{2,1,0:T(8,128)(2,1)} %bitcast.11, s32[2,128]{1,0:T(2,128)} %bitcast.15), custom_call_target="tpu_custom_call" | custom-call | tf_op jit(solution)/shard_map/pallas_call | solution.py:129
  2.3 2.8 %collective-permute-start = (bf16[17,32,128]{2,1,0:T(8,128)(2,1)S(1)}, bf16[17,32,128]{2,1,0:T(8,128)(2,1)S(1)}, u32[]{:S(2)}, u32[]{:S(2)}) collective-permute-start(bf16[17,32,128]{2,1,0:T(8,128)(2,1)S(1)} %get-tuple-element.80), channel_id=1, source_target_pairs={{0,6},{1,7},{2,0},{3,1},{4,2},{5,3},{6,4},{7,5},{8,14},{9,15},{10,... | collective-permute-start | bytes 417800 | tf_op jit(solution)/shard_map/ppermute | solution.py:44
  6.8 2.2 %shard_map.74 = (bf16[6,256,128]{2,1,0:T(8,128)(2,1)S(1)}, bf16[6,256,128]{2,1,0:T(8,128)(2,1)S(1)}, bf16[6,256,128]{2,1,0:T(8,128)(2,1)S(1)}, bf16[6,256,128]{2,1,0:T(8,128)(2,1)S(1)}) custom-call(s32[4]{0:T(128)S(1)} %pad_add_fusion.place, s32[8]{0:T(128)} %owner.5, bf16[256,2560]{1,0:T(8,128)(2,1)} %refs_0_.3, bf16[256,2560]{1,0:T(8,128)(2,1)} %refs_1_.3), custom_call_target="tpu_custom_call" | custom-call | tf_op jit(solution)/shard_map/pallas_call | solution.py:129
  9.0 2.1 %collective-permute-done = bf16[17,32,128]{2,1,0:T(8,128)(2,1)S(1)} collective-permute-done((bf16[17,32,128]{2,1,0:T(8,128)(2,1)S(1)}, bf16[17,32,128]{2,1,0:T(8,128)(2,1)S(1)}, u32[]{:S(2)}, u32[]{:S(2)}) %collective-permute-start) | collective-permute-done | bytes 139296 | tf_op jit(solution)/shard_map/ppermute | solution.py:44
  11.1 2.2 %collective-permute-done.1 = bf16[17,32,128]{2,1,0:T(8,128)(2,1)S(1)} collective-permute-done((bf16[17,32,128]{2,1,0:T(8,128)(2,1)S(1)}, bf16[17,32,128]{2,1,0:T(8,128)(2,1)S(1)}, u32[]{:S(2)}, u32[]{:S(2)}) %collective-permute-start.1) | collective-permute-done | bytes 139296 | tf_op jit(solution)/shard_map/ppermute | solution.py:44
  13.2 1.5 %collective-permute-done.2 = bf16[17,32,128]{2,1,0:T(8,128)(2,1)S(1)} collective-permute-done((bf16[17,32,128]{2,1,0:T(8,128)(2,1)S(1)}, bf16[17,32,128]{2,1,0:T(8,128)(2,1)S(1)}, u32[]{:S(2)}, u32[]{:S(2)}) %collective-permute-start.2) | collective-permute-done | bytes 139296 | tf_op jit(solution)/shard_map/ppermute | solution.py:44
  17.3 2.6 %shard_map.75 = (bf16[4,256,128]{2,1,0:T(8,128)(2,1)S(1)}, bf16[4,256,128]{2,1,0:T(8,128)(2,1)S(1)}, bf16[4,256,128]{2,1,0:T(8,128)(2,1)S(1)}, bf16[4,256,128]{2...) custom-call(s32[4]{0:T(128)S(1)} %pad_add_fusion.place, ...), custom_call_target="tpu_custom_call" | custom-call | tf_op jit(solution)/shard_map/pallas_call | solution.py:129
  19.9 2.6 %shard_map.76 = (s32[4,1,256]{2,1,0:T(1,128)S(1)}, s32[4,52]{1,0:T(4,128)S(1)}) custom-call(s32[4]{0:T(128)S(1)} %pad_add_fusion.place, s32[64]{0:T(128)S(1)} %copy-done), custom_call_target="tpu_custom_call" | custom-call | tf_op jit(solution)/shard_map/pallas_call | solution.py:268
  22.5 4.5 %collective-permute-done.5.refs_1_ = bf16[6,256,128]{2,1,0:T(8,128)(2,1)S(1)} collective-permute-done((bf16[6,256,128]{2,1,0:T(8,128)(2,1)S(1)}, bf16[6,256,128]{2,1,0:T(8,128)(2,1)S(1)}, u32[]{:S(2)}, u32[]{:S(2)}) %collective-permute-start.5) | collective-permute-done | bytes 393248 | tf_op jit(solution)/shard_map/ppermute | solution.py:44
  27.0 2.2 %collective-permute-done.6.refs_2_ = bf16[6,256,128]{2,1,0:T(8,128)(2,1)S(1)} collective-permute-done((bf16[6,256,128]{2,1,0:T(8,128)(2,1)S(1)}, bf16[6,256,128]{2,1,0:T(8,128)(2,1)S(1)}, u32[]{:S(2)}, u32[]{:S(2)}) %collective-permute-start.6) | collective-permute-done | bytes 393248 | tf_op jit(solution)/shard_map/ppermute | solution.py:44
  29.1 7.6 %collective-permute-done.7.refs_3_ = bf16[6,256,128]{2,1,0:T(8,128)(2,1)S(1)} collective-permute-done((bf16[6,256,128]{2,1,0:T(8,128)(2,1)S(1)}, bf16[6,256,128]{2,1,0:T(8,128)(2,1)S(1)}, u32[]{:S(2)}, u32[]{:S(2)}) %collective-permute-start.7) | collective-permute-done | bytes 393248 | tf_op jit(solution)/shard_map/ppermute | solution.py:44
  36.8 1.9 %collective-permute-done.11.far_z.refs_7_ = bf16[4,17,32,128]{3,2,1,0:T(8,128)(2,1)S(1)} collective-permute-done((bf16[4,17,32,128]{3,2,1,0:T(8,128)(2,1)S(1)}, bf16[4,17,32,128]{3,2,1,0:T(8,128)(2,1)S(1)}, u32[]{:S(2)}, u32[]{:S(2)}) %collective-permute-start.11) | collective-permute-done | bytes 557088 | tf_op jit(solution)/shard_map/ppermute | solution.py:44
  39.6 2.3 %shard_map.78.refs_0_ = bf16[4,6,256,128]{3,2,1,0:T(8,128)(2,1)S(1)} custom-call(bf16[6,256,128]{2,1,0:T(8,128)(2,1)S(1)} %get-tuple-element.108.refs_0_, bf16[6,256,128]{2,1,0:T(8,128)(2,1)S(1)} %collective-permute-done.5.refs_1_, bf16[6,256,128]{2,1,0:T(8,128)(2,1)S(1)} %collective-permute-done.6.refs_2_, ...), custom_call_target="tpu_custom_call" | custom-call | tf_op jit(solution)/shard_map/pallas_call | solution.py:197
  42.1 4.8 %collective-permute-start.13 = (bf16[4,6,256,128]{3,2,1,0:T(8,128)(2,1)S(1)}, bf16[4,6,256,128]{3,2,1,0:T(8,128)(2,1)S(1)}, u32[]{:S(2)}, u32[]{:S(2)}) collective-permute-start(bf16[4,6,256,128]{3,2,1,0:T(8,128)(2,1)S(1)} %shard_map.78.refs_0_), channel_id=1, source_target_pairs={{0,8},{1,9},{2,10},{3,11},{4,12},{5,13},{6,14},{7,15},{8,16},{9,17... | collective-permute-start | bytes 4718600 | tf_op jit(solution)/shard_map/ppermute | solution.py:44
  47.0 3.2 %collective-permute-start.8 = (bf16[5,256,128]{2,1,0:T(8,128)(2,1)S(1)}, bf16[5,256,128]{2,1,0:T(8,128)(2,1)S(1)}, u32[]{:S(2)}, u32[]{:S(2)}) collective-permute-start(bf16[5,256,128]{2,1,0:T(8,128)(2,1)S(1)} %get-tuple-element.105), channel_id=1, source_target_pairs={{0,6},{1,7},{2,0},{3,1},{4,2},{5,3},{6,4},{7,5},{8,14},{9,15},{10,... | collective-permute-start | bytes 983048 | tf_op jit(solution)/shard_map/ppermute | solution.py:44
  50.3 14.7 %collective-permute-done.10.refs_3_ = bf16[5,256,128]{2,1,0:T(8,128)(2,1)S(1)} collective-permute-done((bf16[5,256,128]{2,1,0:T(8,128)(2,1)S(1)}, bf16[5,256,128]{2,1,0:T(8,128)(2,1)S(1)}, u32[]{:S(2)}, u32[]{:S(2)}) %collective-permute-start.10) | collective-permute-done | bytes 327712 | tf_op jit(solution)/shard_map/ppermute | solution.py:44
  65.0 3.0 %collective-permute-start.14 = (bf16[4,256,128]{2,1,0:T(8,128)(2,1)S(1)}, bf16[4,256,128]{2,1,0:T(8,128)(2,1)S(1)}, u32[]{:S(2)}, u32[]{:S(2)}) collective-permute-start(bf16[4,256,128]{2,1,0:T(8,128)(2,1)S(1)} %get-tuple-element.125), channel_id=1, source_target_pairs={{0,6},{1,7},{2,0},{3,1},{4,2},{5,3},{6,4},{7,5},{8,14},{9,15},{10,... | collective-permute-start | bytes 786440 | tf_op jit(solution)/shard_map/ppermute | solution.py:44
  68.9 1.8 %shard_map.79.q_hbm = bf16[4,5,256,128]{3,2,1,0:T(8,128)(2,1)S(1)} custom-call(bf16[5,256,128]{2,1,0:T(8,128)(2,1)S(1)} %get-tuple-element.120.refs_0_, bf16[5,256,128]{2,1,0:T(8,128)(2,1)S(1)} %collective-permute-done.8.refs_1_, bf16[5,256,128]{2,1,0:T(8,128)(2,1)S(1)} %collective-permute-done.9.refs_2_, ...), custom_call_target="tpu_custom_call" | custom-call | tf_op jit(solution)/shard_map/pallas_call | solution.py:197
  70.7 9.1 %shard_map.81 = (f32[3,4,8,256]{3,2,1,0:T(8,128)S(1)}, f32[3,4,8,256]{3,2,1,0:T(8,128)S(1)}, f32[3,4,128,256]{3,2,1,0:T(8,128)S(1)}) custom-call(s32[4,52]{1,0:T(4,128)S(1)} %get-tuple-element.102.items, s32[4,1,256]{2,1,0:T(1,128)S(1)} %get-tuple-element.103.begins, bf16[4,5,256,128]{3,2,1,0:T(8,128)(2,1)S(1)} %shard_map.79.q_hbm, ...), custom_call_target="tpu_custom_call" | custom-call | tf_op jit(solution)/shard_map/pallas_call | solution.py:370
  79.8 1.8 %collective-permute-done.16.refs_3_ = bf16[4,256,128]{2,1,0:T(8,128)(2,1)S(1)} collective-permute-done((bf16[4,256,128]{2,1,0:T(8,128)(2,1)S(1)}, bf16[4,256,128]{2,1,0:T(8,128)(2,1)S(1)}, u32[]{:S(2)}, u32[]{:S(2)}) %collective-permute-start.16) | collective-permute-done | bytes 262176 | tf_op jit(solution)/shard_map/ppermute | solution.py:44
  83.5 3.4 %collective-permute-start.17 = (bf16[4,4,256,128]{3,2,1,0:T(8,128)(2,1)S(1)}, bf16[4,4,256,128]{3,2,1,0:T(8,128)(2,1)S(1)}, u32[]{:S(2)}, u32[]{:S(2)}) collective-permute-start(bf16[4,4,256,128]{3,2,1,0:T(8,128)(2,1)S(1)} %shard_map.80.refs_0_), channel_id=1, source_target_pairs={{0,8},{1,9},{2,10},{3,11},{4,12},{5,13},{6,14},{7,15},{8,16},{9,17... | collective-permute-start | bytes 3145736 | tf_op jit(solution)/shard_map/ppermute | solution.py:44
  86.9 7.5 %shard_map.82 = (bf16[3,256,128]{2,1,0:T(8,128)(2,1)S(1)}, bf16[3,256,128]{2,1,0:T(8,128)(2,1)S(1)}, bf16[3,256,128]{2,1,0:T(8,128)(2,1)S(1)}, bf16[3,256,128]{2,1,0:T(8,128)(2,1)S(1)}) custom-call(s32[4,52]{1,0:T(4,128)S(1)} %get-tuple-element.102.items, s32[4,1,256]{2,1,0:T(1,128)S(1)} %get-tuple-element.103.begins, ...), custom_call_target="tpu_custom_call" | custom-call | tf_op jit(solution)/shard_map/pallas_call | solution.py:370
  96.9 6.2 %shard_map.84 = (f32[2,4,8,256]{3,2,1,0:T(8,128)S(1)}, f32[2,4,8,256]{3,2,1,0:T(8,128)S(1)}, f32[2,4,128,256]{3,2,1,0:T(8,128)S(1)}) custom-call(s32[4,52]{1,0:T(4,128)S(1)} %get-tuple-element.102.items, s32[4,1,256]{2,1,0:T(1,128)S(1)} %get-tuple-element.103.begins, bf16[4,5,256,128]{3,2,1,0:T(8,128)(2,1)S(1)} %shard_map.79.q_hbm, ...), custom_call_target="tpu_custom_call" | custom-call | tf_op jit(solution)/shard_map/pallas_call | solution.py:370
  103.1 1.8 %collective-permute-done.20.refs_2_ = bf16[3,256,128]{2,1,0:T(8,128)(2,1)S(1)} collective-permute-done((bf16[3,256,128]{2,1,0:T(8,128)(2,1)S(1)}, bf16[3,256,128]{2,1,0:T(8,128)(2,1)S(1)}, u32[]{:S(2)}, u32[]{:S(2)}) %collective-permute-start.20) | collective-permute-done | bytes 196640 | tf_op jit(solution)/shard_map/ppermute | solution.py:44
  104.9 2.6 %collective-permute-done.21.refs_3_ = bf16[3,256,128]{2,1,0:T(8,128)(2,1)S(1)} collective-permute-done((bf16[3,256,128]{2,1,0:T(8,128)(2,1)S(1)}, bf16[3,256,128]{2,1,0:T(8,128)(2,1)S(1)}, u32[]{:S(2)}, u32[]{:S(2)}) %collective-permute-start.21) | collective-permute-done | bytes 196640 | tf_op jit(solution)/shard_map/ppermute | solution.py:44
  109.0 1.5 %collective-permute-done.17.refs_0_ = bf16[4,4,256,128]{3,2,1,0:T(8,128)(2,1)S(1)} collective-permute-done((bf16[4,4,256,128]{3,2,1,0:T(8,128)(2,1)S(1)}, bf16[4,4,256,128]{3,2,1,0:T(8,128)(2,1)S(1)}, u32[]{:S(2)}, u32[]{:S(2)}) %collective-permute-start.17) | collective-permute-done | bytes 1048608 | tf_op jit(solution)/shard_map/ppermute | solution.py:44
  110.5 2.7 %collective-permute-done.23.refs_1_ = bf16[4,4,256,128]{3,2,1,0:T(8,128)(2,1)S(1)} collective-permute-done((bf16[4,4,256,128]{3,2,1,0:T(8,128)(2,1)S(1)}, bf16[4,4,256,128]{3,2,1,0:T(8,128)(2,1)S(1)}, u32[]{:S(2)}, u32[]{:S(2)}) %collective-permute-start.23) | collective-permute-done | bytes 1048608 | tf_op jit(solution)/shard_map/ppermute | solution.py:44
  113.2 5.2 %shard_map.85 = (bf16[2,256,128]{2,1,0:T(8,128)(2,1)S(1)}, bf16[2,256,128]{2,1,0:T(8,128)(2,1)S(1)}, bf16[2,256,128]{2,1,0:T(8,128)(2,1)S(1)}, bf16[2,256,128]{2,1,0:T(8,128)(2,1)S(1)}) custom-call(s32[4,52]{1,0:T(4,128)S(1)} %get-tuple-element.102.items, s32[4,1,256]{2,1,0:T(1,128)S(1)} %get-tuple-element.103.begins, ...), custom_call_target="tpu_custom_call" | custom-call | tf_op jit(solution)/shard_map/pallas_call | solution.py:370
  119.4 2.0 %collective-permute-start.25 = (bf16[2,256,128]{2,1,0:T(8,128)(2,1)S(1)}, bf16[2,256,128]{2,1,0:T(8,128)(2,1)S(1)}, u32[]{:S(2)}, u32[]{:S(2)}) collective-permute-start(bf16[2,256,128]{2,1,0:T(8,128)(2,1)S(1)} %get-tuple-element.150), channel_id=1, source_target_pairs={{0,4},{1,5},{2,6},{3,7},{4,0},{5,1},{6,2},{7,3},{8,12},{9,13},{10,... | collective-permute-start | bytes 393224 | tf_op jit(solution)/shard_map/ppermute | solution.py:44
  121.4 3.5 %collective-permute-done.24.refs_1_ = bf16[2,256,128]{2,1,0:T(8,128)(2,1)S(1)} collective-permute-done((bf16[2,256,128]{2,1,0:T(8,128)(2,1)S(1)}, bf16[2,256,128]{2,1,0:T(8,128)(2,1)S(1)}, u32[]{:S(2)}, u32[]{:S(2)}) %collective-permute-start.24) | collective-permute-done | bytes 131104 | tf_op jit(solution)/shard_map/ppermute | solution.py:44
  124.8 2.4 %collective-permute-done.25.refs_2_ = bf16[2,256,128]{2,1,0:T(8,128)(2,1)S(1)} collective-permute-done((bf16[2,256,128]{2,1,0:T(8,128)(2,1)S(1)}, bf16[2,256,128]{2,1,0:T(8,128)(2,1)S(1)}, u32[]{:S(2)}, u32[]{:S(2)}) %collective-permute-start.25) | collective-permute-done | bytes 131104 | tf_op jit(solution)/shard_map/ppermute | solution.py:44
  127.3 1.7 %collective-permute-done.26.refs_3_ = bf16[2,256,128]{2,1,0:T(8,128)(2,1)S(1)} collective-permute-done((bf16[2,256,128]{2,1,0:T(8,128)(2,1)S(1)}, bf16[2,256,128]{2,1,0:T(8,128)(2,1)S(1)}, u32[]{:S(2)}, u32[]{:S(2)}) %collective-permute-start.26) | collective-permute-done | bytes 131104 | tf_op jit(solution)/shard_map/ppermute | solution.py:44
  (40 shorter events, 14.7 us)
Async XLA Ops:
  2.3 8.8 %collective-permute-start = (bf16[17,32,128]{2,1,0:T(8,128)(2,1)S(1)}, bf16[17,32,128]{2,1,0:T(8,128)(2,1)S(1)}, u32[]{:S(2)}, u32[]{:S(2)}) collective-permute-start(bf16[17,32,128]{2,1,0:T(8,128)(2,1)S(1)} %get-tuple-element.80), channel_id=1, source_target_pairs={{0,6},{1,7},{2,0},{3,1},{4,2},{5,3},{6,4},{7,5},{8,14},{9,15},{10,... | collective-permute-start | bytes 417800 | tf_op jit(solution)/shard_map/ppermute | solution.py:44
  5.1 8.1 %collective-permute-start.1 = (bf16[17,32,128]{2,1,0:T(8,128)(2,1)S(1)}, bf16[17,32,128]{2,1,0:T(8,128)(2,1)S(1)}, u32[]{:S(2)}, u32[]{:S(2)}) collective-permute-start(bf16[17,32,128]{2,1,0:T(8,128)(2,1)S(1)} %get-tuple-element.86), channel_id=1, source_target_pairs={{0,4},{1,5},{2,6},{3,7},{4,0},{5,1},{6,2},{7,3},{8,12},{9,13},{10,... | collective-permute-start | bytes 417800 | tf_op jit(solution)/shard_map/ppermute | solution.py:44
  5.9 8.8 %collective-permute-start.2 = (bf16[17,32,128]{2,1,0:T(8,128)(2,1)S(1)}, bf16[17,32,128]{2,1,0:T(8,128)(2,1)S(1)}, u32[]{:S(2)}, u32[]{:S(2)}) collective-permute-start(bf16[17,32,128]{2,1,0:T(8,128)(2,1)S(1)} %get-tuple-element.87), channel_id=1, source_target_pairs={{0,2},{1,3},{2,4},{3,5},{4,6},{5,7},{6,0},{7,1},{8,10},{9,11},{10,... | collective-permute-start | bytes 417800 | tf_op jit(solution)/shard_map/ppermute | solution.py:44
  14.8 5.1 %copy-start = (s32[64]{0:T(128)S(1)}, s32[64]{0:T(128)}, u32[]{:S(2)}) copy-start(s32[64]{0:T(128)} %lengths.1) | copy-start | bytes 772
  14.8 21.9 %collective-permute-start.3 = (bf16[4,17,32,128]{3,2,1,0:T(8,128)(2,1)S(1)}, bf16[4,17,32,128]{3,2,1,0:T(8,128)(2,1)S(1)}, u32[]{:S(2)}, u32[]{:S(2)}) collective-permute-start(bf16[4,17,32,128]{3,2,1,0:T(8,128)(2,1)S(1)} %pad_maximum_fusion.near.refs_4_), channel_id=1, source_target_pairs={{0,8},{1,9},{2,10},{3,11},{4,12},{5,13},{6,14},{7,15},{8,0},{9,1},... | collective-permute-start | bytes 1671176 | tf_op jit(solution)/shard_map/ppermute | solution.py:44
  15.0 21.8 %collective-permute-start.4 = (bf16[4,17,32,128]{3,2,1,0:T(8,128)(2,1)S(1)}, bf16[4,17,32,128]{3,2,1,0:T(8,128)(2,1)S(1)}, u32[]{:S(2)}, u32[]{:S(2)}) collective-permute-start(bf16[4,17,32,128]{3,2,1,0:T(8,128)(2,1)S(1)} %pad_maximum_fusion.near.refs_4_), channel_id=1, source_target_pairs={{0,1},{1,0},{2,3},{3,2},{4,5},{5,4},{6,7},{7,6},{8,9},{9,8},{10,11... | collective-permute-start | bytes 1671176 | tf_op jit(solution)/shard_map/ppermute | solution.py:44
  15.0 12.0 %collective-permute-start.5 = (bf16[6,256,128]{2,1,0:T(8,128)(2,1)S(1)}, bf16[6,256,128]{2,1,0:T(8,128)(2,1)S(1)}, u32[]{:S(2)}, u32[]{:S(2)}) collective-permute-start(bf16[6,256,128]{2,1,0:T(8,128)(2,1)S(1)} %get-tuple-element.89), channel_id=1, source_target_pairs={{0,6},{1,7},{2,0},{3,1},{4,2},{5,3},{6,4},{7,5},{8,14},{9,15},{10,... | collective-permute-start | bytes 1179656 | tf_op jit(solution)/shard_map/ppermute | solution.py:44
  15.6 13.5 %collective-permute-start.6 = (bf16[6,256,128]{2,1,0:T(8,128)(2,1)S(1)}, bf16[6,256,128]{2,1,0:T(8,128)(2,1)S(1)}, u32[]{:S(2)}, u32[]{:S(2)}) collective-permute-start(bf16[6,256,128]{2,1,0:T(8,128)(2,1)S(1)} %get-tuple-element.90), channel_id=1, source_target_pairs={{0,4},{1,5},{2,6},{3,7},{4,0},{5,1},{6,2},{7,3},{8,12},{9,13},{10,... | collective-permute-start | bytes 1179656 | tf_op jit(solution)/shard_map/ppermute | solution.py:44
  16.4 20.3 %collective-permute-start.7 = (bf16[6,256,128]{2,1,0:T(8,128)(2,1)S(1)}, bf16[6,256,128]{2,1,0:T(8,128)(2,1)S(1)}, u32[]{:S(2)}, u32[]{:S(2)}) collective-permute-start(bf16[6,256,128]{2,1,0:T(8,128)(2,1)S(1)} %get-tuple-element.91), channel_id=1, source_target_pairs={{0,2},{1,3},{2,4},{3,5},{4,6},{5,7},{6,0},{7,1},{8,10},{9,11},{10,... | collective-permute-start | bytes 1179656 | tf_op jit(solution)/shard_map/ppermute | solution.py:44
  36.8 2.0 %collective-permute-start.11 = (bf16[4,17,32,128]{3,2,1,0:T(8,128)(2,1)S(1)}, bf16[4,17,32,128]{3,2,1,0:T(8,128)(2,1)S(1)}, u32[]{:S(2)}, u32[]{:S(2)}) collective-permute-start(bf16[4,17,32,128]{3,2,1,0:T(8,128)(2,1)S(1)} %collective-permute-done.3.near_z.refs_5_), channel_id=1, source_target_pairs={{0,1},{1,0},{2,3},{3,2},{4,5},{5,4},{6,7},{7,6},{8,9},{9,8},{10,11... | collective-permute-start | bytes 1671176 | tf_op jit(solution)/shard_map/ppermute | solution.py:44
  41.9 23.1 %collective-permute-start.12 = (bf16[4,6,256,128]{3,2,1,0:T(8,128)(2,1)S(1)}, bf16[4,6,256,128]{3,2,1,0:T(8,128)(2,1)S(1)}, u32[]{:S(2)}, u32[]{:S(2)}) collective-permute-start(bf16[4,6,256,128]{3,2,1,0:T(8,128)(2,1)S(1)} %shard_map.78.refs_0_), channel_id=1, source_target_pairs={{0,1},{1,0},{2,3},{3,2},{4,5},{5,4},{6,7},{7,6},{8,9},{9,8},{10,11... | collective-permute-start | bytes 4718600 | tf_op jit(solution)/shard_map/ppermute | solution.py:44
  42.1 40.8 %collective-permute-start.13 = (bf16[4,6,256,128]{3,2,1,0:T(8,128)(2,1)S(1)}, bf16[4,6,256,128]{3,2,1,0:T(8,128)(2,1)S(1)}, u32[]{:S(2)}, u32[]{:S(2)}) collective-permute-start(bf16[4,6,256,128]{3,2,1,0:T(8,128)(2,1)S(1)} %shard_map.78.refs_0_), channel_id=1, source_target_pairs={{0,8},{1,9},{2,10},{3,11},{4,12},{5,13},{6,14},{7,15},{8,16},{9,17... | collective-permute-start | bytes 4718600 | tf_op jit(solution)/shard_map/ppermute | solution.py:44
  46.9 18.0 %collective-permute-start.10 = (bf16[5,256,128]{2,1,0:T(8,128)(2,1)S(1)}, bf16[5,256,128]{2,1,0:T(8,128)(2,1)S(1)}, u32[]{:S(2)}, u32[]{:S(2)}) collective-permute-start(bf16[5,256,128]{2,1,0:T(8,128)(2,1)S(1)} %get-tuple-element.107), channel_id=1, source_target_pairs={{0,2},{1,3},{2,4},{3,5},{4,6},{5,7},{6,0},{7,1},{8,10},{9,11},{10,... | collective-permute-start | bytes 983048 | tf_op jit(solution)/shard_map/ppermute | solution.py:44
  47.0 17.9 %collective-permute-start.8 = (bf16[5,256,128]{2,1,0:T(8,128)(2,1)S(1)}, bf16[5,256,128]{2,1,0:T(8,128)(2,1)S(1)}, u32[]{:S(2)}, u32[]{:S(2)}) collective-permute-start(bf16[5,256,128]{2,1,0:T(8,128)(2,1)S(1)} %get-tuple-element.105), channel_id=1, source_target_pairs={{0,6},{1,7},{2,0},{3,1},{4,2},{5,3},{6,4},{7,5},{8,14},{9,15},{10,... | collective-permute-start | bytes 983048 | tf_op jit(solution)/shard_map/ppermute | solution.py:44
  50.3 14.7 %collective-permute-start.9 = (bf16[5,256,128]{2,1,0:T(8,128)(2,1)S(1)}, bf16[5,256,128]{2,1,0:T(8,128)(2,1)S(1)}, u32[]{:S(2)}, u32[]{:S(2)}) collective-permute-start(bf16[5,256,128]{2,1,0:T(8,128)(2,1)S(1)} %get-tuple-element.106), channel_id=1, source_target_pairs={{0,4},{1,5},{2,6},{3,7},{4,0},{5,1},{6,2},{7,3},{8,12},{9,13},{10,... | collective-permute-start | bytes 983048 | tf_op jit(solution)/shard_map/ppermute | solution.py:44
  65.0 14.8 %collective-permute-start.14 = (bf16[4,256,128]{2,1,0:T(8,128)(2,1)S(1)}, bf16[4,256,128]{2,1,0:T(8,128)(2,1)S(1)}, u32[]{:S(2)}, u32[]{:S(2)}) collective-permute-start(bf16[4,256,128]{2,1,0:T(8,128)(2,1)S(1)} %get-tuple-element.125), channel_id=1, source_target_pairs={{0,6},{1,7},{2,0},{3,1},{4,2},{5,3},{6,4},{7,5},{8,14},{9,15},{10,... | collective-permute-start | bytes 786440 | tf_op jit(solution)/shard_map/ppermute | solution.py:44
  67.9 11.9 %collective-permute-start.15 = (bf16[4,256,128]{2,1,0:T(8,128)(2,1)S(1)}, bf16[4,256,128]{2,1,0:T(8,128)(2,1)S(1)}, u32[]{:S(2)}, u32[]{:S(2)}) collective-permute-start(bf16[4,256,128]{2,1,0:T(8,128)(2,1)S(1)} %get-tuple-element.126), channel_id=1, source_target_pairs={{0,4},{1,5},{2,6},{3,7},{4,0},{5,1},{6,2},{7,3},{8,12},{9,13},{10,... | collective-permute-start | bytes 786440 | tf_op jit(solution)/shard_map/ppermute | solution.py:44
  67.9 13.7 %collective-permute-start.16 = (bf16[4,256,128]{2,1,0:T(8,128)(2,1)S(1)}, bf16[4,256,128]{2,1,0:T(8,128)(2,1)S(1)}, u32[]{:S(2)}, u32[]{:S(2)}) collective-permute-start(bf16[4,256,128]{2,1,0:T(8,128)(2,1)S(1)} %get-tuple-element.127), channel_id=1, source_target_pairs={{0,2},{1,3},{2,4},{3,5},{4,6},{5,7},{6,0},{7,1},{8,10},{9,11},{10,... | collective-permute-start | bytes 786440 | tf_op jit(solution)/shard_map/ppermute | solution.py:44
  82.9 4.0 %collective-permute-start.18 = (bf16[4,6,256,128]{3,2,1,0:T(8,128)(2,1)S(1)}, bf16[4,6,256,128]{3,2,1,0:T(8,128)(2,1)S(1)}, u32[]{:S(2)}, u32[]{:S(2)}) collective-permute-start(bf16[4,6,256,128]{3,2,1,0:T(8,128)(2,1)S(1)} %collective-permute-done.13.refs_0_), channel_id=1, source_target_pairs={{0,1},{1,0},{2,3},{3,2},{4,5},{5,4},{6,7},{7,6},{8,9},{9,8},{10,11... | collective-permute-start | bytes 4718600 | tf_op jit(solution)/shard_map/ppermute | solution.py:44
  83.0 13.9 %collective-permute-start.22 = (bf16[4,4,256,128]{3,2,1,0:T(8,128)(2,1)S(1)}, bf16[4,4,256,128]{3,2,1,0:T(8,128)(2,1)S(1)}, u32[]{:S(2)}, u32[]{:S(2)}) collective-permute-start(bf16[4,4,256,128]{3,2,1,0:T(8,128)(2,1)S(1)} %shard_map.80.refs_0_), channel_id=1, source_target_pairs={{0,1},{1,0},{2,3},{3,2},{4,5},{5,4},{6,7},{7,6},{8,9},{9,8},{10,11... | collective-permute-start | bytes 3145736 | tf_op jit(solution)/shard_map/ppermute | solution.py:44
  83.5 27.0 %collective-permute-start.17 = (bf16[4,4,256,128]{3,2,1,0:T(8,128)(2,1)S(1)}, bf16[4,4,256,128]{3,2,1,0:T(8,128)(2,1)S(1)}, u32[]{:S(2)}, u32[]{:S(2)}) collective-permute-start(bf16[4,4,256,128]{3,2,1,0:T(8,128)(2,1)S(1)} %shard_map.80.refs_0_), channel_id=1, source_target_pairs={{0,8},{1,9},{2,10},{3,11},{4,12},{5,13},{6,14},{7,15},{8,16},{9,17... | collective-permute-start | bytes 3145736 | tf_op jit(solution)/shard_map/ppermute | solution.py:44
  94.5 8.6 %collective-permute-start.19 = (bf16[3,256,128]{2,1,0:T(8,128)(2,1)S(1)}, bf16[3,256,128]{2,1,0:T(8,128)(2,1)S(1)}, u32[]{:S(2)}, u32[]{:S(2)}) collective-permute-start(bf16[3,256,128]{2,1,0:T(8,128)(2,1)S(1)} %get-tuple-element.138), channel_id=1, source_target_pairs={{0,6},{1,7},{2,0},{3,1},{4,2},{5,3},{6,4},{7,5},{8,14},{9,15},{10,... | collective-permute-start | bytes 589832 | tf_op jit(solution)/shard_map/ppermute | solution.py:44
  95.5 9.3 %collective-permute-start.20 = (bf16[3,256,128]{2,1,0:T(8,128)(2,1)S(1)}, bf16[3,256,128]{2,1,0:T(8,128)(2,1)S(1)}, u32[]{:S(2)}, u32[]{:S(2)}) collective-permute-start(bf16[3,256,128]{2,1,0:T(8,128)(2,1)S(1)} %get-tuple-element.139), channel_id=1, source_target_pairs={{0,4},{1,5},{2,6},{3,7},{4,0},{5,1},{6,2},{7,3},{8,12},{9,13},{10,... | collective-permute-start | bytes 589832 | tf_op jit(solution)/shard_map/ppermute | solution.py:44
  96.9 10.6 %collective-permute-start.21 = (bf16[3,256,128]{2,1,0:T(8,128)(2,1)S(1)}, bf16[3,256,128]{2,1,0:T(8,128)(2,1)S(1)}, u32[]{:S(2)}, u32[]{:S(2)}) collective-permute-start(bf16[3,256,128]{2,1,0:T(8,128)(2,1)S(1)} %get-tuple-element.140), channel_id=1, source_target_pairs={{0,2},{1,3},{2,4},{3,5},{4,6},{5,7},{6,0},{7,1},{8,10},{9,11},{10,... | collective-permute-start | bytes 589832 | tf_op jit(solution)/shard_map/ppermute | solution.py:44
  110.5 2.7 %collective-permute-start.23 = (bf16[4,4,256,128]{3,2,1,0:T(8,128)(2,1)S(1)}, bf16[4,4,256,128]{3,2,1,0:T(8,128)(2,1)S(1)}, u32[]{:S(2)}, u32[]{:S(2)}) collective-permute-start(bf16[4,4,256,128]{3,2,1,0:T(8,128)(2,1)S(1)} %collective-permute-done.17.refs_0_), channel_id=1, source_target_pairs={{0,1},{1,0},{2,3},{3,2},{4,5},{5,4},{6,7},{7,6},{8,9},{9,8},{10,11... | collective-permute-start | bytes 3145736 | tf_op jit(solution)/shard_map/ppermute | solution.py:44
  118.4 6.4 %collective-permute-start.24 = (bf16[2,256,128]{2,1,0:T(8,128)(2,1)S(1)}, bf16[2,256,128]{2,1,0:T(8,128)(2,1)S(1)}, u32[]{:S(2)}, u32[]{:S(2)}) collective-permute-start(bf16[2,256,128]{2,1,0:T(8,128)(2,1)S(1)} %get-tuple-element.149), channel_id=1, source_target_pairs={{0,6},{1,7},{2,0},{3,1},{4,2},{5,3},{6,4},{7,5},{8,14},{9,15},{10,... | collective-permute-start | bytes 393224 | tf_op jit(solution)/shard_map/ppermute | solution.py:44
  119.4 7.9 %collective-permute-start.25 = (bf16[2,256,128]{2,1,0:T(8,128)(2,1)S(1)}, bf16[2,256,128]{2,1,0:T(8,128)(2,1)S(1)}, u32[]{:S(2)}, u32[]{:S(2)}) collective-permute-start(bf16[2,256,128]{2,1,0:T(8,128)(2,1)S(1)} %get-tuple-element.150), channel_id=1, source_target_pairs={{0,4},{1,5},{2,6},{3,7},{4,0},{5,1},{6,2},{7,3},{8,12},{9,13},{10,... | collective-permute-start | bytes 393224 | tf_op jit(solution)/shard_map/ppermute | solution.py:44
  121.4 7.6 %collective-permute-start.26 = (bf16[2,256,128]{2,1,0:T(8,128)(2,1)S(1)}, bf16[2,256,128]{2,1,0:T(8,128)(2,1)S(1)}, u32[]{:S(2)}, u32[]{:S(2)}) collective-permute-start(bf16[2,256,128]{2,1,0:T(8,128)(2,1)S(1)} %get-tuple-element.151), channel_id=1, source_target_pairs={{0,2},{1,3},{2,4},{3,5},{4,6},{5,7},{6,0},{7,1},{8,10},{9,11},{10,... | collective-permute-start | bytes 393224 | tf_op jit(solution)/shard_map/ppermute | solution.py:44
